TPU v7x, 32 devices: a whole 2x2x4 slice. The times are simulated.
32 devices in a mesh: groups: 2 (over x), row: 16 (over z, y, core).
Axes of the slice: x: 2, y: 2, z: 4, core: 2. Of those that a mesh axis runs over, the one named last changes fastest.
Arguments:
- charges: bfloat16 [65536, 128], P(('groups', 'row')), parts along dimension 0, may hold values from -6 to 6
- cotangent: bfloat16 [65536, 128], P(('groups', 'row')), parts along dimension 0, may hold values from -6 to 6
- spread_weight: bfloat16 [1024, 128, 960], P(('groups', 'row')), parts along dimension 0, may hold values from -0.5 to 0.5
- atom_list: int32 [1024, 128], P(('groups', 'row')), parts along dimension 0, may hold values from -1 to 2047, as said below
- filter_modes: float32 [256, 256, 4], replicated, may hold values from 0.25 to 2
- gain: float32 [128], replicated, may hold values from 0.5 to 2
Outputs:
- charge_grad: bfloat16 [65536, 128], P(('groups', 'row')), parts along dimension 0
- filter_grad: float32 [256, 256, 8], P('row', None, 'groups'), parts along dimension 2
- gain_grad: float32 [256], P('groups'), parts along dimension 0
There are 2 independent parts, one for each index of `groups`. A program takes and returns all parts, laid end to end along the dimension named above; an argument that names none is the same for every part. Nothing has to cross between parts.
Inputs may be any that keep to these rules, and one draw needn't show every extreme that they name: `atom_list`: entries other than -1 index the 2048 atoms of the index of row that holds the pencil; each such atom stands in exactly one slot of that block of 32 pencils, and in every block some pencil has all 128 slots occupied.
All inputs are finite; a program needn't handle non-finite values.
Results may differ from a plain program's by a relative error of at most 0.0078.
Values may be sent and summed in bfloat16 or wider, within the bound.
A program may use at most 192 MiB of HBM per device.

v0:
```python
import math

import jax
import jax.numpy as jnp
from jax import lax
from jax.sharding import PartitionSpec as P

NX = 256
NY = 256
NZ = 4
C = 128
H = 2
BX = 8


def from_behind(value, axis, steps):
    count = lax.axis_size(axis)
    pairs = [(source, (source + steps) % count) for source in range(count)]
    return lax.ppermute(value, axis, pairs)


def with_halo(cells, sides, width):
    for axis, dim in sides:
        count = lax.axis_size(axis)
        head = lax.slice_in_dim(cells, 0, width, axis=dim)
        tail = lax.slice_in_dim(cells, cells.shape[dim] - width, cells.shape[dim], axis=dim)
        cells = jnp.concatenate(
            [
                lax.ppermute(tail, axis, [(i, (i + 1) % count) for i in range(count)]),
                cells,
                lax.ppermute(head, axis, [((i + 1) % count, i) for i in range(count)]),
            ],
            axis=dim,
        )
    return cells


def wave_tables(length):
    counter = jnp.arange(length, dtype=jnp.int32)
    turns = counter[:, None] * counter[None, :] % length
    angle = turns.astype(jnp.float32) * (2.0 * math.pi / length)
    factor = 1.0 / math.sqrt(length)
    return (
        (jnp.cos(angle) * factor).astype(jnp.bfloat16),
        (jnp.sin(angle) * factor).astype(jnp.bfloat16),
    )


def local(charges, cotangent, spread_weight, atom_list, filter_modes, gain):
    row_count = lax.axis_size("row")
    pencils, slot_count, ext_cells = spread_weight.shape
    y_local = NY // row_count
    x_local = NX // row_count
    span_x = BX + 2 * H
    span_y = y_local + 2 * H
    occupied = atom_list >= 0
    slot_rows = jnp.where(occupied, atom_list, 0)
    slot_live = occupied.astype(jnp.bfloat16)[..., None]

    def spread(source):
        gathered = jnp.take(source, slot_rows, axis=0) * slot_live
        extended = jnp.einsum(
            "pse,psc->pec", spread_weight, gathered, preferred_element_type=jnp.float32
        )
        extended = extended.reshape(pencils, span_x, span_y, NZ, C)
        interior = extended[:, H : H + BX]
        interior = interior.at[:, BX - H :].add(jnp.roll(extended[:, :H], -1, axis=0))
        interior = interior.at[:, :H].add(jnp.roll(extended[:, H + BX :], 1, axis=0))
        return interior.reshape(NX, span_y, NZ, C)

    charge_ext = spread(charges)
    grad_ext = spread(cotangent)
    upper = jnp.stack([charge_ext[:, H + y_local :], grad_ext[:, H + y_local :]])
    lower = jnp.stack([charge_ext[:, :H], grad_ext[:, :H]])
    from_below = from_behind(upper, "row", 1)
    from_above = from_behind(lower, "row", -1)

    def settle(extended, below, above):
        interior = extended[:, H : H + y_local]
        interior = interior.at[:, :H].add(below).at[:, y_local - H :].add(above)
        return interior.astype(jnp.bfloat16)

    density = settle(charge_ext, from_below[0], from_above[0])
    spread_grad = settle(grad_ext, from_below[1], from_above[1])
    cos_x, sin_x = wave_tables(NX)
    cos_y, sin_y = wave_tables(NY)
    forward_x = jnp.concatenate([cos_x, -sin_x], axis=0)
    inverse_x = jnp.concatenate([cos_x, -sin_x], axis=1)
    highest = lax.Precision.HIGHEST

    def transform_x(source):
        section = jnp.dot(forward_x, source.reshape(NX, -1), preferred_element_type=jnp.float32)
        return section.astype(jnp.bfloat16).reshape(2, NX, y_local, NZ, C)

    density_x, spread_x = (
        lax.all_to_all(transform_x(density), "row", split_axis=1, concat_axis=2, tiled=True),
        lax.all_to_all(transform_x(spread_grad), "row", split_axis=1, concat_axis=2, tiled=True),
    )

    def transform_y(operand):
        cos_part = jnp.einsum("ky,axyzc->axkzc", cos_y, operand, preferred_element_type=jnp.float32)
        sin_part = jnp.einsum("ky,axyzc->axkzc", sin_y, operand, preferred_element_type=jnp.float32)
        return (cos_part[0] + sin_part[1], cos_part[1] - sin_part[0])

    density_re, density_im = transform_y(density_x)
    spread_re, spread_im = transform_y(spread_x)
    offset = lax.axis_index("row") * x_local
    filter_block = lax.dynamic_slice_in_dim(filter_modes, offset, x_local, 0)
    mode_product = density_re * spread_re + density_im * spread_im
    filter_grad = jnp.einsum("xyzc,c->xyz", mode_product, gain, precision=highest)
    own_terms = jnp.einsum("xyzc,xyz->c", mode_product, filter_block, precision=highest)
    gain_grad = lax.psum(own_terms, "row")
    scaling = filter_block[..., None] * gain
    filtered = jnp.stack([scaling * spread_re, scaling * spread_im]).astype(jnp.bfloat16)
    cos_back = jnp.einsum("ky,axyzc->axkzc", cos_y, filtered, preferred_element_type=jnp.float32)
    sin_back = jnp.einsum("ky,axyzc->axkzc", sin_y, filtered, preferred_element_type=jnp.float32)
    back_y = jnp.stack([cos_back[0] - sin_back[1], cos_back[1] + sin_back[0]]).astype(jnp.bfloat16)
    spatial = lax.all_to_all(back_y, "row", split_axis=2, concat_axis=1, tiled=True)
    rho_grad = jnp.dot(inverse_x, spatial.reshape(2 * NX, -1), preferred_element_type=jnp.float32)
    rho_grad = rho_grad.astype(jnp.bfloat16).reshape(NX, y_local, NZ, C)
    padded = with_halo(rho_grad, (("row", 1),), H)
    pieces = padded.reshape(pencils, BX, span_y, NZ, C)
    lower_x = jnp.roll(pieces, 1, axis=0)[:, BX - H :]
    upper_x = jnp.roll(pieces, -1, axis=0)[:, :H]
    extended = jnp.concatenate([lower_x, pieces, upper_x], axis=1).reshape(pencils, ext_cells, C)
    slot_values = jnp.einsum(
        "pse,pec->psc", spread_weight, extended, preferred_element_type=jnp.float32
    )
    atom_count = charges.shape[0]
    targets = jnp.where(occupied, atom_list, atom_count)
    charge_grad = (
        jnp.zeros((atom_count, C), jnp.float32)
        .at[targets.reshape(-1)]
        .add(slot_values.reshape(-1, C), mode="drop")
    )
    return (charge_grad.astype(jnp.bfloat16), filter_grad, gain_grad)


def solution(mesh):
    placed = (
        P(("groups", "row"), None),
        P(("groups", "row"), None),
        P(("groups", "row"), None, None),
        P(("groups", "row"), None),
        P(),
        P(),
    )
    return jax.shard_map(
        local,
        mesh=mesh,
        in_specs=placed,
        out_specs=(P(("groups", "row"), None), P("row", None, "groups"), P("groups")),
        check_vma=False,
    )
```

profile of v0, /device:TPU:1, one launch (start us, length us, event | category | flops | bytes accessed | tf_op | source)
XLA Modules:
  0.0 1062.5 jit_solution(9336385425401791897)
XLA Ops:
  2.2 12.1 %gather_fusion = bf16[4096,128]{1,0:T(8,128)(2,1)S(1)} fusion(bf16[2048,128]{1,0:T(8,128)(2,1)} %param.25, s32[4096]{0:T(1024)S(1)} %bitcast_clamp_fusion), kind=kCustom, calls=%fused_computation.clone | custom fusion | bytes 2113536 | tf_op jit(solution)/shard_map/jit(_take)/gather | solution.py:61
  27.0 10.9 %slice.464 = f32[32,8,20,4,128]{4,3,2,1,0:T(4,128)} slice(f32[32,12,20,4,128]{4,3,2,1,0:T(4,128)} %bitcast.144), slice={[0:32], [2:10], [0:20], [0:4], [0:128]} | slice | bytes 20971520 | tf_op jit(solution)/shard_map/slice | solution.py:66
  38.0 12.1 %gather_fusion.1 = bf16[4096,128]{1,0:T(8,128)(2,1)S(1)} fusion(bf16[2048,128]{1,0:T(8,128)(2,1)S(1)} %copy-done.3, s32[4096]{0:T(1024)S(1)} %bitcast_clamp_fusion), kind=kCustom, calls=%fused_computation.1.clone | custom fusion | bytes 2113536 | tf_op jit(solution)/shard_map/jit(_take)/gather | solution.py:61
  62.8 10.8 %slice.473 = f32[32,8,20,4,128]{4,3,2,1,0:T(4,128)} slice(f32[32,12,20,4,128]{4,3,2,1,0:T(4,128)} %bitcast.148), slice={[0:32], [2:10], [0:20], [0:4], [0:128]} | slice | bytes 20971520 | tf_op jit(solution)/shard_map/slice | solution.py:66
  98.1 10.5 slice.471
  108.6 10.4 slice.501
  131.6 20.6 %collective-permute-done.1 = f32[2,256,2,4,128]{4,3,2,1,0:T(4,128)S(1)} collective-permute-done((f32[2,256,2,4,128]{4,3,2,1,0:T(4,128)S(1)}, f32[2,256,2,4,128]{4,3,2,1,0:T(4,128)S(1)}, u32[]{:S(2)}, u32[]{:S(2)}) %collective-permute-start.1) | collective-permute-done | bytes 2097184 | tf_op jit(solution)/shard_map/ppermute | solution.py:19
  179.2 14.3 %reshape.415 = bf16[2,256,16,4,128]{4,3,2,1,0:T(4,128)(2,1)} reshape(bf16[512,8192]{1,0:T(8,128)(2,1)} %convolution_convert_fusion) | data formatting | bytes 16777216 | tf_op jit(solution)/shard_map/reshape | solution.py:93
  193.4 9.3 copy.67
  233.2 14.4 %reshape.407 = bf16[2,256,16,4,128]{4,3,2,1,0:T(4,128)(2,1)} reshape(bf16[512,8192]{1,0:T(8,128)(2,1)} %convolution_convert_fusion.1) | data formatting | bytes 16777216 | tf_op jit(solution)/shard_map/reshape | solution.py:93
  247.5 9.3 copy.51
  256.8 104.0 %all-to-all-done.2 = bf16[2,256,16,4,128]{4,2,3,0,1:T(8,128)(2,1)} async-done(((bf16[2,256,16,4,128]{4,2,3,0,1:T(8,128)(2,1)}), bf16[2,256,16,4,128]{4,2,3,0,1:T(8,128)(2,1)}, u32[]{:S(2)}, u32[]{:S(2)}) %all-to-all-start.2) | async-done | bytes 8388640 | tf_op jit(solution)/shard_map/all_to_all | solution.py:96
  360.9 36.3 %all-to-all-start = ((bf16[2,256,16,4,128]{4,2,3,0,1:T(8,128)(2,1)}), bf16[2,256,16,4,128]{4,2,3,0,1:T(8,128)(2,1)}, u32[]{:S(2)}, u32[]{:S(2)}) async-start(bf16[2,256,16,4,128]{4,2,3,0,1:T(8,128)(2,1)} %copy.51), calls=%async_computation | async-start | bytes 16777216 | tf_op jit(solution)/shard_map/all_to_all | solution.py:97
  406.2 12.6 %convolution_bitcast_fusion = f32[2,16,256,4,128]{2,4,3,1,0:T(8,128)} fusion(bf16[2,16,256,4,128]{4,2,3,1,0:T(8,128)(2,1)} %bitcast.138), kind=kOutput, calls=%fused_computation.28 | convolution fusion | flops 2148532224 | bytes 25165824 | tf_op jit(solution)/shard_map/ky,axyzc->axkzc/dot_general | solution.py:102
  418.8 9.1 convolution_bitcast_fusion.1
  427.8 120.3 %all-to-all-done = bf16[2,256,16,4,128]{4,2,3,0,1:T(8,128)(2,1)} async-done(((bf16[2,256,16,4,128]{4,2,3,0,1:T(8,128)(2,1)}), bf16[2,256,16,4,128]{4,2,3,0,1:T(8,128)(2,1)}, u32[]{:S(2)}, u32[]{:S(2)}) %all-to-all-start) | async-done | bytes 8388640 | tf_op jit(solution)/shard_map/all_to_all | solution.py:97
  557.0 13.1 %convolution_bitcast_fusion.4 = f32[2,16,256,4,128]{2,4,3,1,0:T(8,128)} fusion(bf16[2,16,256,4,128]{4,2,3,1,0:T(8,128)(2,1)} %bitcast.140), kind=kOutput, calls=%fused_computation.32 | convolution fusion | flops 2148532224 | bytes 25165824 | tf_op jit(solution)/shard_map/ky,axyzc->axkzc/dot_general | solution.py:102
  570.1 9.0 convolution_bitcast_fusion.5
  579.1 26.4 %fusion.2 = (bf16[1,16,256,4,128]{2,4,3,1,0:T(8,128)(2,1)S(1)}, bf16[1,16,256,4,128]{2,4,3,1,0:T(8,128)(2,1)S(1)}, f32[16,256,4,128]{1,3,2,0:T(8,128)}) fusion(f32[128]{0:T(128)S(1)} %copy-done.15, f32[16,256,4]{1,2,0:T(4,128)S(1)} %constant_dynamic-slice_fusion, f32[2,16,256,4,128]{2,4,3,1,0:T(8,128)} %convolution_bitcast_fusion.4, ...), kind=kLoop, calls=%fused_computation.12 | loop fusion | flops 25165824 | bytes 83952128 | tf_op jit(solution)/shard_map/convert.2
  621.4 14.4 %fusion.9 = (bf16[1,16,256,4,128]{2,4,3,1,0:T(8,128)(2,1)S(1)}, bf16[1,16,256,4,128]{2,4,3,1,0:T(8,128)(2,1)}) fusion(f32[2,16,256,4,128]{2,4,3,1,0:T(8,128)} %convolution_bitcast_fusion.2, f32[2,16,256,4,128]{2,4,3,1,0:T(8,128)} %convolution_bitcast_fusion.3), kind=kLoop, calls=%fused_computation.23 | loop fusion | flops 8388608 | bytes 41943040 | tf_op jit(solution)/shard_map/convert
  642.1 14.6 %copy.56 = bf16[2,16,256,4,128]{4,3,1,0,2:T(4,128)(2,1)} copy(bf16[2,16,256,4,128]{2,4,3,1,0:T(8,128)(2,1)} %pad_maximum_fusion.3) | data formatting | bytes 16777216 | tf_op jit(solution)/shard_map/stack | solution.py:117
  656.7 36.3 %all-to-all-start.1 = ((bf16[2,16,256,4,128]{4,3,1,0,2:T(4,128)(2,1)}), bf16[2,16,256,4,128]{4,3,1,0,2:T(4,128)(2,1)}, u32[]{:S(2)}, u32[]{:S(2)}) async-start(bf16[2,16,256,4,128]{4,3,1,0,2:T(4,128)(2,1)} %copy.56), calls=%async_computation.1 | async-start | bytes 16777216 | tf_op jit(solution)/shard_map/all_to_all | solution.py:118
  693.0 151.1 %all-to-all-done.1 = bf16[2,16,256,4,128]{4,3,1,0,2:T(4,128)(2,1)} async-done(((bf16[2,16,256,4,128]{4,3,1,0,2:T(4,128)(2,1)}), bf16[2,16,256,4,128]{4,3,1,0,2:T(4,128)(2,1)}, u32[]{:S(2)}, u32[]{:S(2)}) %all-to-all-start.1) | async-done | bytes 8388640 | tf_op jit(solution)/shard_map/all_to_all | solution.py:118
  844.1 16.3 %copy.57 = bf16[2,16,256,4,128]{4,2,3,1,0:T(8,128)(2,1)} copy(bf16[2,16,256,4,128]{4,3,1,0,2:T(4,128)(2,1)} %all-to-all-done.1) | data formatting | bytes 16777216 | tf_op jit(solution)/shard_map/all_to_all | solution.py:118
  860.4 18.3 %copy.58 = bf16[2,16,16,16,4,128]{5,4,3,2,1,0:T(4,128)(2,1)} copy(bf16[2,16,16,16,4,128]{5,3,1,4,2,0:T(8,128)(2,1)} %bitcast.156) | data formatting | bytes 16777216 | tf_op jit(solution)/shard_map/all_to_all | solution.py:118
  878.7 14.5 %reshape.408 = bf16[512,8192]{1,0:T(8,128)(2,1)} reshape(bf16[2,16,16,16,4,128]{5,4,3,2,1,0:T(4,128)(2,1)} %copy.58) | data formatting | bytes 16777216 | tf_op jit(solution)/shard_map/reshape | solution.py:119
  910.3 11.2 %collective-permute-start.2 = (bf16[256,2,4,128]{3,0,2,1:T(8,128)(2,1)S(1)}, bf16[256,2,4,128]{3,0,2,1:T(8,128)(2,1)S(1)}, u32[]{:S(2)}, u32[]{:S(2)}) collective-permute-start(bf16[256,2,4,128]{3,0,2,1:T(8,128)(2,1)S(1)} %copy.88), channel_id=1, source_target_pairs={{0,1},{1,2},{2,3},{3,4},{4,5},{5,6},{6,7},{7,8},{8,9},{9,10},{10,1... | collective-permute-start | bytes 1572872 | tf_op jit(solution)/shard_map/ppermute | solution.py:29
  937.9 49.0 %psum.7 = f32[128]{0:T(128)} all-reduce(f32[128]{0:T(128)S(1)} %convolution_bitcast_fusion.6), channel_id=1, replica_groups=mesh['groups'=2,'row'=16] {'row'}, use_global_device_ids=true, to_apply=%region_1.3 | all-reduce | flops 128 | bytes 1024 | tf_op jit(solution)/shard_map/psum | solution.py:112
  1000.4 9.5 slice_bitcast_fusion.1
  1011.0 12.7 %fusion = bf16[32,12,20,4,128]{4,1,3,2,0:T(8,128)(2,1)S(1)} fusion(bf16[1,8,20,4,128]{4,1,3,2,0:T(8,128)(2,1)S(1)} %get-tuple-element.118, bf16[1,8,20,4,128]{4,1,3,2,0:T(8,128)(2,1)S(1)} %get-tuple-element.117, bf16[32,8,16,4,128]{4,1,3,2,0:T(8,128)(2,1)} %bitcast.158, bf16[256,2,4,128]{3,0,2,1:T(8,128)(2,1)S(1)} %collective-permute-done.2, ...), kind=kLoop, calls=%fused_computation.8 | loop fusion | flops 55050240 | bytes 23592960 | tf_op jit(solution)/shard_map/concatenate | solution.py:125
  1029.0 9.3 fusion.93
  1038.3 22.9 %scatter_custom_fusion = f32[2048,128]{1,0:T(8,128)S(1)} fusion(s32[4096]{0:T(1024)S(1)} %bitcast.164, f32[4096,128]{1,0:T(8,128)} %bitcast.161, f32[]{:T(128)} %constant.222.clone.1), kind=kCustom, calls=%fused_computation.73 | custom fusion | flops 524288 | bytes 1049088 | tf_op jit(solution)/shard_map/scatter-add | solution.py:134
  (87 shorter events, 215.3 us)
Async XLA Ops:
  0.6 396.6 %copy-start = (f32[256,256,4]{1,2,0:T(4,128)S(1)}, f32[256,256,4]{1,2,0:T(4,128)}, u32[]{:S(2)}) copy-start(f32[256,256,4]{1,2,0:T(4,128)} %param.28) | copy-start | bytes 3145732
  20.0 7.0 copy-start.4
  27.0 10.9 %copy-start.3 = (bf16[2048,128]{1,0:T(8,128)(2,1)S(1)}, bf16[2048,128]{1,0:T(8,128)(2,1)}, u32[]{:S(2)}) copy-start(bf16[2048,128]{1,0:T(8,128)(2,1)} %param.24) | copy-start | bytes 1572868
  55.8 7.0 copy-start.5
  73.5 10.8 %copy-start.6 = (f32[32,8,20,4,128]{4,3,2,1,0:T(4,128)S(1)}, f32[32,8,20,4,128]{4,3,2,1,0:T(4,128)}, u32[]{:S(2)}) copy-start(f32[32,8,20,4,128]{4,3,2,1,0:T(4,128)} %slice.473) | copy-start | bytes 31457284
  73.6 10.8 %copy-start.9 = (f32[31,2,20,4,128]{4,3,2,1,0:T(4,128)S(1)}, f32[31,2,20,4,128]{4,3,2,1,0:T(4,128)}, u32[]{:S(2)}) copy-start(f32[31,2,20,4,128]{4,3,2,1,0:T(4,128)} %get-tuple-element.108) | copy-start | bytes 7618564
  78.6 8.6 copy-start.8
  88.5 4.0 copy-start.7
  95.2 25.9 %collective-permute-start = (f32[2,256,2,4,128]{4,3,2,1,0:T(4,128)S(1)}, f32[2,256,2,4,128]{4,3,2,1,0:T(4,128)S(1)}, u32[]{:S(2)}, u32[]{:S(2)}) collective-permute-start(f32[2,256,2,4,128]{4,3,2,1,0:T(4,128)S(1)} %pad_maximum_fusion.6), channel_id=1, source_target_pairs={{0,1},{1,2},{2,3},{3,4},{4,5},{5,6},{6,7},{7,8},{8,9},{9,10},{10,1... | collective-permute-start | bytes 6291464 | tf_op jit(solution)/shard_map/ppermute | solution.py:19
  125.6 26.7 %collective-permute-start.1 = (f32[2,256,2,4,128]{4,3,2,1,0:T(4,128)S(1)}, f32[2,256,2,4,128]{4,3,2,1,0:T(4,128)S(1)}, u32[]{:S(2)}, u32[]{:S(2)}) collective-permute-start(f32[2,256,2,4,128]{4,3,2,1,0:T(4,128)S(1)} %pad_maximum_fusion.7), channel_id=1, source_target_pairs={{0,15},{1,0},{2,1},{3,2},{4,3},{5,4},{6,5},{7,6},{8,7},{9,8},{10,9... | collective-permute-start | bytes 6291464 | tf_op jit(solution)/shard_map/ppermute | solution.py:19
  130.6 94.7 %copy-start.10 = (bf16[256,256]{1,0:T(8,128)(2,1)}, bf16[256,256]{1,0:T(8,128)(2,1)S(1)}, u32[]{:S(2)}) copy-start(bf16[256,256]{1,0:T(8,128)(2,1)S(1)} %fusion.47) | copy-start | bytes 393220
  131.6 93.7 %copy-start.12 = (bf16[256,256]{1,0:T(8,128)(2,1)}, bf16[256,256]{1,0:T(8,128)(2,1)S(1)}, u32[]{:S(2)}) copy-start(bf16[256,256]{1,0:T(8,128)(2,1)S(1)} %multiply_convert_fusion.1) | copy-start | bytes 393220
  202.7 158.1 %all-to-all-start.2 = ((bf16[2,256,16,4,128]{4,2,3,0,1:T(8,128)(2,1)}), bf16[2,256,16,4,128]{4,2,3,0,1:T(8,128)(2,1)}, u32[]{:S(2)}, u32[]{:S(2)}) async-start(bf16[2,256,16,4,128]{4,2,3,0,1:T(8,128)(2,1)} %copy.67), calls=%async_computation.2 | async-start | bytes 16777216 | tf_op jit(solution)/shard_map/all_to_all | solution.py:96
  360.9 187.3 %all-to-all-start = ((bf16[2,256,16,4,128]{4,2,3,0,1:T(8,128)(2,1)}), bf16[2,256,16,4,128]{4,2,3,0,1:T(8,128)(2,1)}, u32[]{:S(2)}, u32[]{:S(2)}) async-start(bf16[2,256,16,4,128]{4,2,3,0,1:T(8,128)(2,1)} %copy.51), calls=%async_computation | async-start | bytes 16777216 | tf_op jit(solution)/shard_map/all_to_all | solution.py:97
  406.2 12.6 %copy-start.1 = (bf16[2,16,16,16,4,128]{5,3,2,4,1,0:T(8,128)(2,1)S(1)}, bf16[2,16,16,16,4,128]{5,3,2,4,1,0:T(8,128)(2,1)}, u32[]{:S(2)}) copy-start(bf16[2,16,16,16,4,128]{5,3,2,4,1,0:T(8,128)(2,1)} %copy.69) | copy-start | bytes 25165828
  557.0 13.1 %copy-start.2 = (bf16[2,16,16,16,4,128]{5,3,2,4,1,0:T(8,128)(2,1)S(1)}, bf16[2,16,16,16,4,128]{5,3,2,4,1,0:T(8,128)(2,1)}, u32[]{:S(2)}) copy-start(bf16[2,16,16,16,4,128]{5,3,2,4,1,0:T(8,128)(2,1)} %copy.53) | copy-start | bytes 25165828
  570.1 9.0 copy-start.15
  656.7 36.3 %copy-start.14 = (s32[32,128]{1,0:T(8,128)S(1)}, s32[32,128]{1,0:T(8,128)}, u32[]{:S(2)}) copy-start(s32[32,128]{1,0:T(8,128)} %param.27) | copy-start | bytes 49156
  656.7 187.4 %all-to-all-start.1 = ((bf16[2,16,256,4,128]{4,3,1,0,2:T(4,128)(2,1)}), bf16[2,16,256,4,128]{4,3,1,0,2:T(4,128)(2,1)}, u32[]{:S(2)}, u32[]{:S(2)}) async-start(bf16[2,16,256,4,128]{4,3,1,0,2:T(4,128)(2,1)} %copy.56), calls=%async_computation.1 | async-start | bytes 16777216 | tf_op jit(solution)/shard_map/all_to_all | solution.py:118
  878.7 14.5 %copy-start.11 = (bf16[256,256]{1,0:T(8,128)(2,1)S(1)}, bf16[256,256]{1,0:T(8,128)(2,1)}, u32[]{:S(2)}) copy-start(bf16[256,256]{1,0:T(8,128)(2,1)} %copy-done.10) | copy-start | bytes 393220
  878.7 14.5 %copy-start.13 = (bf16[256,256]{1,0:T(8,128)(2,1)S(1)}, bf16[256,256]{1,0:T(8,128)(2,1)}, u32[]{:S(2)}) copy-start(bf16[256,256]{1,0:T(8,128)(2,1)} %copy-done.12) | copy-start | bytes 393220
  910.3 81.5 %collective-permute-start.2 = (bf16[256,2,4,128]{3,0,2,1:T(8,128)(2,1)S(1)}, bf16[256,2,4,128]{3,0,2,1:T(8,128)(2,1)S(1)}, u32[]{:S(2)}, u32[]{:S(2)}) collective-permute-start(bf16[256,2,4,128]{3,0,2,1:T(8,128)(2,1)S(1)} %copy.88), channel_id=1, source_target_pairs={{0,1},{1,2},{2,3},{3,4},{4,5},{5,6},{6,7},{7,8},{8,9},{9,10},{10,1... | collective-permute-start | bytes 1572872 | tf_op jit(solution)/shard_map/ppermute | solution.py:29
  987.0 12.6 %collective-permute-start.3 = (bf16[256,2,4,128]{3,0,2,1:T(8,128)(2,1)S(1)}, bf16[256,2,4,128]{3,0,2,1:T(8,128)(2,1)S(1)}, u32[]{:S(2)}, u32[]{:S(2)}) collective-permute-start(bf16[256,2,4,128]{3,0,2,1:T(8,128)(2,1)S(1)} %copy.89), channel_id=1, source_target_pairs={{1,0},{2,1},{3,2},{4,3},{5,4},{6,5},{7,6},{8,7},{9,8},{10,9},{11,1... | collective-permute-start | bytes 1572872 | tf_op jit(solution)/shard_map/ppermute | solution.py:31
where the time goes:
time: 1070 us; the launch traced here: 1060 us
  waiting for transfers between devices  398 us (37%)
  local copies, waits for them, and re-layouts  266 us (25%)
  other arithmetic  126 us (12%)
  matrix products  119 us (11%)
  starting transfers between devices  103 us (10%)
  blocking collectives  49 us (5%)
    all_to_all x1, waiting for transfers between devices, local(): lax.all_to_all(back_y, 'row', split_axis=2, concat_axis=1, tiled=True)  151 us
    all_to_all x1, waiting for transfers between devices, local(): lax.all_to_all(transform_x(spread_grad), 'row', split_axis=1, concat_axis...  120 us
    all_to_all x1, waiting for transfers between devices, local(): lax.all_to_all(transform_x(density), 'row', split_axis=1, concat_axis=2,...  104 us
    psum x1, blocking collectives, local(): gain_grad = lax.psum(own_terms, 'row')  49 us
    reshape x4, local copies, waits for them, and re-layouts, transform_x(): return section.astype(jnp.bfloat16).reshape(2, NX, y_local, NZ, C)  47.3 us
    another operation x2, other arithmetic  40.8 us
    all_to_all x1, starting transfers between devices, local(): lax.all_to_all(transform_x(spread_grad), 'row', split_axis=1, concat_axis...  36.3 us
    all_to_all x1, starting transfers between devices, local(): lax.all_to_all(back_y, 'row', split_axis=2, concat_axis=1, tiled=True)  36.3 us
  transfers between devices with their start and end apart: 7, of which 5 were waited for; matrix products, arithmetic and copies ran while one was open for 12% of the time, Pallas kernels for 0%

commit v1 on v0

v1 whole, which is shorter than its diff:
```python
import functools
import math

import jax
import jax.numpy as jnp
import ml_dtypes
import numpy as np
from jax import lax
from jax.experimental import pallas as pl
from jax.experimental.pallas import tpu as pltpu
from jax.sharding import PartitionSpec as P

NX = 256
NY = 256
NZ = 4
C = 128
H = 2
BX = 8
HR = H * NZ
VMEM_LIMIT = 58 * 1024 * 1024
BF = jnp.bfloat16
F32 = jnp.float32


def wave_tables(length):
    counter = np.arange(length)
    turns = counter[:, None] * counter[None, :] % length
    angle = turns.astype(np.float32) * np.float32(2.0 * math.pi / length)
    factor = np.float32(1.0 / math.sqrt(length))
    return np.cos(angle) * factor, np.sin(angle) * factor


def packed_x_table(rows):
    cos_x, sin_x = wave_tables(NX)
    half = NX // 2
    re = cos_x[:half].copy()
    im = -sin_x[:half]
    im[0] = cos_x[half]
    k_local = half // rows
    both = np.stack([re.reshape(rows, k_local, NX), im.reshape(rows, k_local, NX)], axis=1)
    return both.reshape(NX, NX)


def params(steps=1):
    return pltpu.CompilerParams(
        dimension_semantics=("arbitrary",) * steps, vmem_limit_bytes=VMEM_LIMIT
    )


def full(shape):
    return pl.BlockSpec(shape, lambda *_: (0,) * len(shape))


def dot(a, b):
    return jnp.dot(a, b, preferred_element_type=F32)


def spread_kernel(group, span, atom_ref, source_ref, weight_ref, out_ref, first, second):
    step = pl.program_id(0)
    atoms = source_ref.shape[0]
    slots = weight_ref.shape[2]

    @pl.when(step == 0)
    def _():
        zero = jnp.zeros((2 * H * span, C), F32)
        first[0 : 2 * H * span] = zero
        second[0 : 2 * H * span] = zero

    lane = lax.broadcasted_iota(jnp.int32, (slots, 128), 1).astype(F32)
    marks = []
    for j in range(group):
        held = jnp.broadcast_to(atom_ref[step * group + j], (128, slots)).T
        marks.append(
            jnp.concatenate(
                [(held == lane + float(a)).astype(F32).astype(BF) for a in range(0, atoms, 128)], axis=1
            )
        )
    gathered = dot(jnp.concatenate(marks, axis=0), source_ref[...]).astype(BF)
    for j in range(group):
        ext = dot(weight_ref[j], gathered[j * slots : (j + 1) * slots])
        base = pl.multiple_of((step * group + j) * (BX * span), 8)
        for half, total in enumerate((first, second)):
            part = ext[:, half * C : (half + 1) * C]
            total[pl.ds(base, 2 * H * span)] += part[: 2 * H * span]
            total[pl.ds(pl.multiple_of(base + 2 * H * span, 8), BX * span)] = part[2 * H * span :]

    @pl.when(step == pl.num_programs(0) - 1)
    def _():
        for half, total in enumerate((first, second)):
            total[NX * span : (NX + H) * span] += total[0 : H * span]
            total[H * span : 2 * H * span] += total[(NX + H) * span : (NX + 2 * H) * span]

            def move(r, _):
                out_ref[r, :, half * C : (half + 1) * C] = total[
                    pl.ds(H * span + r, NX, stride=span), :
                ].astype(BF)
                return 0

            lax.fori_loop(0, span, move, 0)


def spread(atom_rows, source, weight, span):
    pencils, ext, slots = weight.shape
    group = 4
    return pl.pallas_call(
        functools.partial(spread_kernel, group, span),
        grid=(pencils // group,),
        in_specs=[
            full(atom_rows.shape),
            full(source.shape),
            pl.BlockSpec((group, ext, slots), lambda i: (i, 0, 0)),
        ],
        out_specs=full((span, NX, 2 * C)),
        out_shape=jax.ShapeDtypeStruct((span, NX, 2 * C), BF),
        scratch_shapes=[pltpu.VMEM(((NX + 2 * H) * span, C), F32)] * 2,
        compiler_params=params(),
        cost_estimate=pl.CostEstimate(flops=7 * 10**9, bytes_accessed=24 * 10**6, transcendentals=0),
    )(atom_rows, source, weight)


def forward_x_kernel(y_local, table_ref, ext_ref, below_ref, above_ref, out_ref, wide):
    inner = y_local * NZ

    def put(r, value):
        place = (r % NZ) * y_local + r // NZ
        wide[pl.ds(place, NX, stride=inner + 1), :] = value

    def run(start, stop, extra):
        def body(i, _):
            r = start + 2 * i
            values = []
            for u in range(2):
                value = ext_ref[HR + r + u]
                if extra is not None:
                    value = (value.astype(F32) + extra(r + u).astype(F32)).astype(BF)
                values.append(value)
            result = dot(table_ref[...], jnp.concatenate(values, axis=1))
            put(r, result[:, :C])
            put(r + 1, result[:, C:])
            return 0

        if stop > start:
            lax.fori_loop(0, (stop - start) // 2, body, 0)

    run(0, HR, lambda r: below_ref[r])
    run(HR, inner - HR, None)
    run(inner - HR, inner, lambda r: above_ref[r - (inner - HR)])

    def cast(i, _):
        for u in range(8):
            k = i * 8 + u
            out_ref[pl.ds(pl.multiple_of(k * inner, 16), inner)] = wide[
                pl.ds(k * (inner + 1), inner)
            ].astype(BF)
        return 0

    lax.fori_loop(0, NX // 8, cast, 0)


def forward_x(table, ext, below, above, which, y_local):
    span = ext.shape[0]
    inner = y_local * NZ
    pick = lambda n: pl.BlockSpec((n, NX, C), lambda i: (0, 0, which))
    return pl.pallas_call(
        functools.partial(forward_x_kernel, y_local),
        grid=(1,),
        in_specs=[full((NX, NX)), pick(span), pick(HR), pick(HR)],
        out_specs=full((NX * inner, C)),
        out_shape=jax.ShapeDtypeStruct((NX * inner, C), BF),
        scratch_shapes=[pltpu.VMEM((NX * (inner + 1), C), F32)],
        compiler_params=params(),
        cost_estimate=pl.CostEstimate(flops=10**9, bytes_accessed=12 * 10**6, transcendentals=0),
    )(table, ext, below, above)


def modes_kernel(fwd_ref, inv_ref, flag_ref, gain_ref, filt_ref, last_ref, density_ref, grad_ref,
                 back_ref, fgrad_ref, flast_ref, ggrad_ref):
    step = pl.program_id(0)
    gain = gain_ref[...]

    @pl.when(step == 0)
    def _():
        ggrad_ref[...] = jnp.zeros_like(ggrad_ref)

    def load(ref, part, z):
        return ref[:, part, 0, z].reshape(NY, C)

    def store(part, z, value):
        back_ref[:, part, 0, z] = value.astype(BF).reshape(back_ref.shape[0], back_ref.shape[4], C)

    def run(parts, weight):
        weight = jnp.concatenate([weight, jnp.zeros((128 - NZ, NY), F32)], axis=0).T
        columns, filtered, total = [], [], jnp.zeros((1, C), F32)
        for z in range(NZ):
            d_re, d_im, g_re, g_im = parts(z)
            stacked = jnp.concatenate(
                [jnp.concatenate([d_re, g_re], axis=1), jnp.concatenate([d_im, g_im], axis=1)], axis=0
            )
            hat = dot(fwd_ref[...], stacked)
            dr, di = hat[:NY, :C], hat[NY:, :C]
            gr, gi = hat[:NY, C:], hat[NY:, C:]
            product = dr * gr + di * gi
            filt = weight[:, z : z + 1]
            columns.append(jnp.sum(product * gain, axis=1, keepdims=True))
            total = total + jnp.sum(product * filt, axis=0, keepdims=True)
            scaling = filt * gain
            filtered.append(
                jnp.concatenate([(scaling * gr).astype(BF), (scaling * gi).astype(BF)], axis=0)
            )
        ggrad_ref[...] += jnp.broadcast_to(total, ggrad_ref.shape)
        back = []
        for z in range(0, NZ, 2):
            both = dot(inv_ref[...], jnp.concatenate(filtered[z : z + 2], axis=1))
            back += [both[:, :C], both[:, C:]]
        columns.append(jnp.zeros((NY, 128 - NZ), F32))
        return jnp.concatenate(columns, axis=1).T[:NZ], back

    @pl.when(step > 0)
    def _():
        def parts(z):
            return (load(density_ref, 0, z), load(density_ref, 1, z),
                    load(grad_ref, 0, z), load(grad_ref, 1, z))

        columns, back = run(parts, filt_ref[0])
        fgrad_ref[0] = columns
        for z in range(NZ):
            store(0, z, back[z][:NY])
            store(1, z, back[z][NY:])

    @pl.when(step == 0)
    def _():
        flag = flag_ref[...]
        other = 1.0 - flag
        flag_b, other_b = flag.astype(BF), other.astype(BF)

        def parts(z):
            return (load(density_ref, 0, z), load(density_ref, 1, z) * other_b,
                    load(grad_ref, 0, z), load(grad_ref, 1, z) * other_b)

        columns, back = run(parts, filt_ref[0])
        fgrad_ref[0] = columns

        def last_parts(z):
            zero = jnp.zeros((NY, C), BF)
            return (load(density_ref, 1, z) * flag_b, zero, load(grad_ref, 1, z) * flag_b, zero)

        columns, last = run(last_parts, last_ref[...])
        flast_ref[...] = columns
        for z in range(NZ):
            store(0, z, back[z][:NY])
            store(1, z, back[z][NY:] * other + last[z][:NY] * flag)


def modes(fwd, inv, flag, gain, filt, last, density, grad):
    sources, _, k_local, _, y_rows, _ = density.shape
    block = pl.BlockSpec((sources, 2, 1, NZ, y_rows, C), lambda i: (0, 0, i, 0, 0, 0))
    column = pl.BlockSpec((1, NZ, NY), lambda i: (i, 0, 0))
    return pl.pallas_call(
        modes_kernel,
        grid=(k_local,),
        in_specs=[full(fwd.shape), full(inv.shape), full((1, C)), full((1, C)), column,
                  full((NZ, NY)), block, block],
        out_specs=[block, column, full((NZ, NY)), full((8, C))],
        out_shape=[
            jax.ShapeDtypeStruct(density.shape, BF),
            jax.ShapeDtypeStruct((k_local, NZ, NY), F32),
            jax.ShapeDtypeStruct((NZ, NY), F32),
            jax.ShapeDtypeStruct((8, C), F32),
        ],
        compiler_params=params(),
        cost_estimate=pl.CostEstimate(flops=10 * 10**9, bytes_accessed=14 * 10**6, transcendentals=0),
    )(fwd, inv, flag, gain, filt, last, density, grad)


def inverse_x_kernel(y_local, table_ref, in_ref, out_ref, wide, result):
    inner = y_local * NZ

    def widen(i, _):
        for u in range(8):
            k = i * 8 + u
            wide[pl.ds(k * (inner + 1), inner)] = in_ref[
                pl.ds(pl.multiple_of(k * inner, 16), inner)
            ].astype(F32)
        return 0

    lax.fori_loop(0, NX // 8, widen, 0)

    def body(i, _):
        values = []
        for u in range(2):
            r = 2 * i + u
            place = (r % NZ) * y_local + r // NZ
            values.append(wide[pl.ds(place, NX, stride=inner + 1), :].astype(BF))
        both = dot(table_ref[...], jnp.concatenate(values, axis=1))
        result[pl.ds(2 * i, NX, stride=inner + 1), :] = both[:, :C]
        result[pl.ds(2 * i + 1, NX, stride=inner + 1), :] = both[:, C:]
        return 0

    lax.fori_loop(0, inner // 2, body, 0)

    def cast(i, _):
        for u in range(8):
            x = i * 8 + u
            out_ref[pl.ds(pl.multiple_of(x * inner, 16), inner)] = result[
                pl.ds(x * (inner + 1), inner)
            ].astype(BF)
        return 0

    lax.fori_loop(0, NX // 8, cast, 0)


def inverse_x(table, back, y_local):
    shape = (NX * y_local * NZ, C)
    return pl.pallas_call(
        functools.partial(inverse_x_kernel, y_local),
        grid=(1,),
        in_specs=[full((NX, NX)), full(shape)],
        out_specs=full(shape),
        out_shape=jax.ShapeDtypeStruct(shape, BF),
        scratch_shapes=[pltpu.VMEM((NX * (y_local * NZ + 1), C), F32)] * 2,
        compiler_params=params(),
        cost_estimate=pl.CostEstimate(flops=10**9, bytes_accessed=8 * 10**6, transcendentals=0),
    )(table, back)


def collect_kernel(group, span, atom_ref, weight_ref, rho_ref, below_ref, above_ref, out_ref, ext, total):
    step = pl.program_id(0)
    atoms = total.shape[0]
    slots = weight_ref.shape[2]

    @pl.when(step == 0)
    def _():
        def build(i, _):
            x = (i + NX - H) % NX
            rows = jnp.concatenate(
                [below_ref[x].astype(F32), rho_ref[x].astype(F32), above_ref[x].astype(F32)], axis=0
            )
            ext[pl.ds(pl.multiple_of(i * span, 16), span)] = rows.astype(BF)
            return 0

        lax.fori_loop(0, NX + 2 * H, build, 0)
        total[...] = jnp.zeros_like(total)

    marks, values = [], []
    row = lax.broadcasted_iota(jnp.int32, (atoms, slots), 0).astype(F32)
    for j in range(group):
        p = step * group + j
        cells = ext[pl.ds(pl.multiple_of(p * (BX * span), 16), (BX + 2 * H) * span)]
        value = lax.dot_general(
            weight_ref[j], cells, (((0,), (0,)), ((), ())), preferred_element_type=F32
        )
        values.append(value.astype(BF))
        marks.append((row == atom_ref[p]).astype(F32).astype(BF))
    total[...] += dot(jnp.concatenate(marks, axis=1), jnp.concatenate(values, axis=0))

    @pl.when(step == pl.num_programs(0) - 1)
    def _():
        out_ref[...] = total[...].astype(BF)


def collect(atom_rows, weight, rho, below, above, atoms, span):
    pencils, ext, slots = weight.shape
    group = 4
    return pl.pallas_call(
        functools.partial(collect_kernel, group, span),
        grid=(pencils // group,),
        in_specs=[
            full(atom_rows.shape),
            pl.BlockSpec((group, ext, slots), lambda i: (i, 0, 0)),
            full(rho.shape),
            full(below.shape),
            full(above.shape),
        ],
        out_specs=full((atoms, C)),
        out_shape=jax.ShapeDtypeStruct((atoms, C), BF),
        scratch_shapes=[
            pltpu.VMEM(((NX + 2 * H) * span, C), BF),
            pltpu.VMEM((atoms, C), F32),
        ],
        compiler_params=params(),
        cost_estimate=pl.CostEstimate(flops=4 * 10**9, bytes_accessed=14 * 10**6, transcendentals=0),
    )(atom_rows, weight, rho, below, above)


def from_behind(value, axis, steps):
    count = lax.axis_size(axis)
    return lax.ppermute(value, axis, [(source, (source + steps) % count) for source in range(count)])


def flip_modes(modes_rows):
    return jnp.roll(jnp.flip(modes_rows, axis=-1), 1, axis=-1)


def local(charges, cotangent, spread_weight, atom_list, filter_modes, gain):
    rows = lax.axis_size("row")
    me = lax.axis_index("row")
    pencils = spread_weight.shape[0]
    atoms = charges.shape[0]
    y_local = NY // rows
    half = NX // 2
    k_local = half // rows
    inner = y_local * NZ
    span = inner + 2 * HR
    cos_y, sin_y = wave_tables(NY)
    packed = packed_x_table(rows)
    as_table = lambda t: jnp.asarray(t.astype(ml_dtypes.bfloat16))
    fwd_x = as_table(packed)
    inv_x = as_table(packed.T)
    fwd_y = as_table(np.block([[cos_y, sin_y], [-sin_y, cos_y]]))
    inv_y = as_table(np.block([[cos_y, -sin_y], [sin_y, cos_y]]))
    atom_rows = atom_list.astype(F32)[:, None, :]
    weight = spread_weight.transpose(0, 2, 1)

    ext = spread(atom_rows, jnp.concatenate([charges, cotangent], axis=1), weight, span)
    below = from_behind(ext[span - HR :], "row", 1)
    above = from_behind(ext[:HR], "row", -1)

    def exchange(cells):
        return lax.all_to_all(cells, "row", split_axis=0, concat_axis=0, tiled=True)

    def by_owner(grid):
        got = exchange(grid.reshape(rows, 2 * k_local, NZ, y_local, C))
        got = got.reshape(rows, 2, k_local, NZ, y_local, C)
        if y_local % 16:
            got = got.transpose(1, 2, 3, 0, 4, 5).reshape(1, 2, k_local, NZ, NY, C)
        return got

    density = by_owner(forward_x(fwd_x, ext, below, above, 0, y_local))
    grad = by_owner(forward_x(fwd_x, ext, below, above, 1, y_local))

    own = me * k_local
    filter_modes = filter_modes.transpose(0, 2, 1)
    straight = lax.dynamic_slice_in_dim(filter_modes, own, k_local, 0)
    mirrored = flip_modes(filter_modes)
    ks = own + jnp.arange(k_local)
    opposite = jnp.take(mirrored, (NX - ks) % NX, axis=0)
    filt = straight + jnp.where((ks == 0)[:, None, None], 0.0, opposite)
    flag = jnp.broadcast_to((me == 0).astype(F32), (1, C))
    back, fgrad, flast, ggrad = modes(
        fwd_y, inv_y, flag, gain[None, :], filt, filter_modes[half], density, grad
    )
    small = jnp.concatenate([fgrad.reshape(-1, C), flast.reshape(-1, C), ggrad], axis=0)
    shared = lax.all_gather(small, "row")
    if y_local % 16:
        back = back.reshape(2, k_local, NZ, rows, y_local, C).transpose(3, 0, 1, 2, 4, 5)
    back = exchange(back.reshape(rows, 2 * k_local, NZ, y_local, C))
    rho = inverse_x(inv_x, back.reshape(NX * inner, C), y_local).reshape(NX, inner, C)
    below = from_behind(rho[:, inner - HR :], "row", 1)
    above = from_behind(rho[:, :HR], "row", -1)
    charge_grad = collect(atom_rows, weight, rho, below, above, atoms, span)

    plane = NY * NZ // C
    body = shared[:, : k_local * plane].reshape(half, NZ, NY)
    last = shared[0, k_local * plane : (k_local + 1) * plane].reshape(1, NZ, NY)
    gain_grad = jnp.sum(shared[:, (k_local + 1) * plane], axis=0)
    known = jnp.concatenate([body, last], axis=0)
    mine = me * (NX // rows) + jnp.arange(NX // rows)
    picked = jnp.take(known, jnp.where(mine <= half, mine, NX - mine), axis=0)
    filter_grad = jnp.where((mine <= half)[:, None, None], picked, flip_modes(picked))
    return (charge_grad, filter_grad.transpose(0, 2, 1), gain_grad)


def solution(mesh):
    placed = (
        P(("groups", "row"), None),
        P(("groups", "row"), None),
        P(("groups", "row"), None, None),
        P(("groups", "row"), None),
        P(),
        P(),
    )
    return jax.shard_map(
        local,
        mesh=mesh,
        in_specs=placed,
        out_specs=(P(("groups", "row"), None), P("row", None, "groups"), P("groups")),
        check_vma=False,
    )
```

time: 1070 us -> 448 us (0.42)
  local copies, waits for them, and re-layouts: 266 us -> 11.3 us
  waiting for transfers between devices: 398 us -> 175 us
  matrix products: 119 us -> 0 us
  other arithmetic: 126 us -> 7.53 us
  Pallas kernels: 0 us -> 100 us
  starting transfers between devices: 103 us -> 62.4 us
  blocking collectives: 49 us -> 88.9 us
    all_to_all x3, waiting for transfers between devices: 375 us -> 137 us  [exchange(): return lax.all_to_all(cells, 'row', split_axis=0, concat_axis=0, tiled=True)]
    dot_general x14 -> x0, matrix products: 119 us -> none  [the longest x2 25.7 us: transform_y(): jnp.einsum('ky,axyzc->axkzc', sin_y, operand, preferred_element_type=jnp....]
    pallas_call x0 -> x6, Pallas kernels: none -> 100 us  [the longest x1 35.6 us: spread(): pl.pallas_call(functools.partial(spread_kernel, group, span), grid=(penci...]
    all_gather x0 -> x1, blocking collectives: none -> 88.9 us  [local(): shared = lax.all_gather(small, 'row')]
    reshape x8 -> x3, local copies, waits for them, and re-layouts: 85.2 us -> 0.27 us  [the longest x1 0.25 us: local(): body = shared[:, :k_local * plane].reshape(half, NZ, NY)]
    slice x11 -> x8, local copies, waits for them, and re-layouts: 60.5 us -> 4.6 us  [the longest x1 1.68 us: local(): above = from_behind(ext[:HR], 'row', -1)]
    all_to_all x4 -> x0, local copies, waits for them, and re-layouts: 52.5 us -> none  [the longest x2 34.7 us: local(): lax.all_to_all(back_y, 'row', split_axis=2, concat_axis=1, tiled=True)]
    psum x1 -> x0, blocking collectives: 49 us -> none  [local(): gain_grad = lax.psum(own_terms, 'row')]
  transfers between devices with their start and end apart: 7 -> 7, of which waited for: 5 -> 6; matrix products, arithmetic and copies ran while one was open for 12% -> 2% of each run, Pallas kernels for 0% -> 3%
where the time goes in v1:
time: 448 us; the launch traced here: 447 us
  waiting for transfers between devices  175 us (39%)
  Pallas kernels  100 us (22%)
  blocking collectives  88.9 us (20%)
  starting transfers between devices  62.4 us (14%)
  local copies, waits for them, and re-layouts  11.3 us (3%)
  other arithmetic  7.53 us (2%)
    all_to_all x3, waiting for transfers between devices, exchange(): return lax.all_to_all(cells, 'row', split_axis=0, concat_axis=0, tiled=True)  137 us
    all_gather x1, blocking collectives, local(): shared = lax.all_gather(small, 'row')  88.9 us
    all_to_all x3, starting transfers between devices, exchange(): return lax.all_to_all(cells, 'row', split_axis=0, concat_axis=0, tiled=True)  44.4 us
    ppermute x4, waiting for transfers between devices, from_behind(): lax.ppermute(value, axis, [(source, (source + steps) % count) for source...  37.8 us
    pallas_call x1, Pallas kernels, spread(): pl.pallas_call(functools.partial(spread_kernel, group, span), grid=(penci...  35.6 us
    pallas_call x2, Pallas kernels, forward_x(): pl.pallas_call(functools.partial(forward_x_kernel, y_local), grid=(1,), i...  23.4 us
    ppermute x4, starting transfers between devices, from_behind(): lax.ppermute(value, axis, [(source, (source + steps) % count) for source...  17.9 us
    pallas_call x1, Pallas kernels, collect(): pl.pallas_call(functools.partial(collect_kernel, group, span), grid=(penc...  16.3 us
  transfers between devices with their start and end apart: 7, of which 6 were waited for; matrix products, arithmetic and copies ran while one was open for 2% of the time, Pallas kernels for 3%

profile of v1, /device:TPU:1, one launch (start us, length us, event | category | flops | bytes accessed | tf_op | source)
XLA Modules:
  0.0 446.5 jit_solution(17509173033456730227)
XLA Ops:
  0.6 1.3 convert_element_type.6
  1.9 2.3 pad_maximum_fusion.1.source_ref
  4.2 35.6 %shard_map.121.ext_ref = bf16[80,256,256]{2,1,0:T(8,128)(2,1)} custom-call(f32[32,1,128]{2,1,0:T(1,128)} %bitcast.37, bf16[2048,256]{1,0:T(8,128)(2,1)} %pad_maximum_fusion.1.source_ref, bf16[32,960,128]{2,1,0:T(8,128)(2,1)} %bitcast.39), custom_call_target="tpu_custom_call" | custom-call | flops 7000000000 | bytes 24000000 | tf_op jit(solution)/shard_map/pallas_call | solution.py:105
  39.8 1.7 fusion.7
  41.5 2.7 collective-permute-start
  44.2 23.0 %collective-permute-done.below_ref = bf16[8,256,256]{2,1,0:T(8,128)(2,1)S(1)} collective-permute-done((bf16[8,256,256]{2,1,0:T(8,128)(2,1)S(1)}, bf16[8,256,256]{2,1,0:T(8,128)(2,1)S(1)}, u32[]{:S(2)}, u32[]{:S(2)}) %collective-permute-start) | collective-permute-done | bytes 1048608 | tf_op jit(solution)/shard_map/ppermute | solution.py:387
  67.2 2.5 collective-permute-done.1.above_ref
  69.6 1.0 copy-done.1
  70.7 11.7 %shard_map.123 = bf16[16384,128]{1,0:T(8,128)(2,1)} custom-call(bf16[256,256]{1,0:T(8,128)(2,1)} %constant.67.clone.table_ref, bf16[80,256,256]{2,1,0:T(8,128)(2,1)} %shard_map.121.ext_ref, bf16[8,256,256]{2,1,0:T(8,128)(2,1)} %copy-done, bf16[8,256,256]{2,1,0:T(8,128)(2,1)} %copy-done.1), custom_call_target="tpu_custom_call" | custom-call | flops 1000000000 | bytes 12000000 | tf_op jit(solution)/shard_map/pallas_call | solution.py:164
  82.4 5.7 %all-to-all-start.1 = ((bf16[16,16,4,16,128]{4,3,2,1,0:T(8,128)(2,1)}), bf16[16,16,4,16,128]{4,3,2,1,0:T(8,128)(2,1)}, u32[]{:S(2)}, u32[]{:S(2)}) async-start(bf16[16,16,4,16,128]{4,3,2,1,0:T(8,128)(2,1)} %bitcast.25), calls=%async_computation.1 | async-start | bytes 8388608 | tf_op jit(solution)/shard_map/all_to_all | solution.py:419
  88.1 11.7 %shard_map.122 = bf16[16384,128]{1,0:T(8,128)(2,1)} custom-call(bf16[256,256]{1,0:T(8,128)(2,1)} %constant.67.clone.table_ref, bf16[80,256,256]{2,1,0:T(8,128)(2,1)} %shard_map.121.ext_ref, bf16[8,256,256]{2,1,0:T(8,128)(2,1)} %copy-done, bf16[8,256,256]{2,1,0:T(8,128)(2,1)} %copy-done.1), custom_call_target="tpu_custom_call" | custom-call | flops 1000000000 | bytes 12000000 | tf_op jit(solution)/shard_map/pallas_call | solution.py:164
  99.8 66.4 %all-to-all-done.1 = bf16[16,16,4,16,128]{4,3,2,1,0:T(8,128)(2,1)} async-done(((bf16[16,16,4,16,128]{4,3,2,1,0:T(8,128)(2,1)}), bf16[16,16,4,16,128]{4,3,2,1,0:T(8,128)(2,1)}, u32[]{:S(2)}, u32[]{:S(2)}) %all-to-all-start.1) | async-done | bytes 4194336 | tf_op jit(solution)/shard_map/all_to_all | solution.py:419
  166.2 19.4 %all-to-all-start = ((bf16[16,16,4,16,128]{4,3,2,1,0:T(8,128)(2,1)}), bf16[16,16,4,16,128]{4,3,2,1,0:T(8,128)(2,1)}, u32[]{:S(2)}, u32[]{:S(2)}) async-start(bf16[16,16,4,16,128]{4,3,2,1,0:T(8,128)(2,1)} %bitcast.24), calls=%async_computation | async-start | bytes 8388608 | tf_op jit(solution)/shard_map/all_to_all | solution.py:419
  185.6 0.6 slice.67
  186.2 0.9 slice.66
  187.1 1.3 reverse.4
  188.5 0.6 slice.80
  189.1 1.6 pad_maximum_fusion
  191.4 0.6 slice_bitcast_fusion.last_ref
  192.0 0.7 bitcast_add_fusion.filt_ref
  192.7 71.1 %all-to-all-done = bf16[16,16,4,16,128]{4,3,2,1,0:T(8,128)(2,1)} async-done(((bf16[16,16,4,16,128]{4,3,2,1,0:T(8,128)(2,1)}), bf16[16,16,4,16,128]{4,3,2,1,0:T(8,128)(2,1)}, u32[]{:S(2)}, u32[]{:S(2)}) %all-to-all-start) | async-done | bytes 4194336 | tf_op jit(solution)/shard_map/all_to_all | solution.py:419
  264.2 13.2 %shard_map.124 = (bf16[16,2,8,4,16,128]{5,4,3,2,1,0:T(8,128)(2,1)}, f32[8,4,256]{2,1,0:T(4,128)}, f32[4,256]{1,0:T(4,128)}, f32[8,128]{1,0:T(8,128)}) custom-call(bf16[512,512]{1,0:T(8,128)(2,1)} %constant.69.clone.fwd_ref, bf16[512,512]{1,0:T(8,128)(2,1)} %constant.70.clone.inv_ref, f32[1,128]{1,0:T(1,128)} %broadcast_in_dim.52.flag_ref, ...), custom_call_target="tpu_custom_call" | custom-call | flops 10000000000 | bytes 14000000 | tf_op jit(solution)/shard_map/pallas_call | solution.py:258
  277.5 19.3 %all-to-all-start.2 = ((bf16[16,16,4,16,128]{4,3,2,1,0:T(8,128)(2,1)}), bf16[16,16,4,16,128]{4,3,2,1,0:T(8,128)(2,1)}, u32[]{:S(2)}, u32[]{:S(2)}) async-start(bf16[16,16,4,16,128]{4,3,2,1,0:T(8,128)(2,1)} %bitcast.28), calls=%async_computation.2 | async-start | bytes 8388608 | tf_op jit(solution)/shard_map/all_to_all | solution.py:419
  296.9 88.9 %all-gather = f32[1280,128]{1,0:T(8,128)S(1)} all-gather(f32[80,128]{1,0:T(8,128)S(1)} %pad_maximum_fusion.3), channel_id=2, replica_groups=mesh['groups'=2,'row'=16] {'row'}, dimensions={0}, use_global_device_ids=true | all-gather | bytes 696320 | tf_op jit(solution)/shard_map/all_gather | solution.py:443
  386.8 11.9 %shard_map.125 = bf16[16384,128]{1,0:T(8,128)(2,1)} custom-call(bf16[256,256]{1,0:T(8,128)(2,1)} %constant.68.clone.table_ref, bf16[16384,128]{1,0:T(8,128)(2,1)} %bitcast.12.in_ref), custom_call_target="tpu_custom_call" | custom-call | flops 1000000000 | bytes 8000000 | tf_op jit(solution)/shard_map/pallas_call | solution.py:314
  398.7 1.3 fusion.8
  400.0 15.2 %collective-permute-start.2 = (bf16[256,8,128]{2,1,0:T(8,128)(2,1)S(1)}, bf16[256,8,128]{2,1,0:T(8,128)(2,1)S(1)}, u32[]{:S(2)}, u32[]{:S(2)}) collective-permute-start(bf16[256,8,128]{2,1,0:T(8,128)(2,1)S(1)} %get-tuple-element.14), channel_id=1, source_target_pairs={{0,1},{1,2},{2,3},{3,4},{4,5},{5,6},{6,7},{7,8},{8,9},{9,10},{10,1... | collective-permute-start | bytes 1572872 | tf_op jit(solution)/shard_map/ppermute | solution.py:387
  416.4 0.8 fusion
  417.1 9.8 %collective-permute-done.2.below_ref = bf16[256,8,128]{2,1,0:T(8,128)(2,1)S(1)} collective-permute-done((bf16[256,8,128]{2,1,0:T(8,128)(2,1)S(1)}, bf16[256,8,128]{2,1,0:T(8,128)(2,1)S(1)}, u32[]{:S(2)}, u32[]{:S(2)}) %collective-permute-start.2) | collective-permute-done | bytes 524320 | tf_op jit(solution)/shard_map/ppermute | solution.py:387
  427.0 2.5 collective-permute-done.3.above_ref
  429.5 0.8 copy-done.7
  430.3 16.3 %shard_map.126 = bf16[2048,128]{1,0:T(8,128)(2,1)} custom-call(f32[32,1,128]{2,1,0:T(1,128)} %bitcast.38, bf16[32,960,128]{2,1,0:T(8,128)(2,1)} %bitcast.40, bf16[256,64,128]{2,1,0:T(8,128)(2,1)} %bitcast.27, bf16[256,8,128]{2,1,0:T(8,128)(2,1)} %copy-done.6, bf16[256,8,128]{2,1,0:T(8,128)(2,1)} %copy-done.7), custom_call_target="tpu_custom_call" | custom-call | flops 4000000000 | bytes 14000000 | tf_op jit(solution)/shard_map/pallas_call | solution.py:364
  (41 shorter events, 3.3 us)
Async XLA Ops:
  41.5 25.7 %collective-permute-start = (bf16[8,256,256]{2,1,0:T(8,128)(2,1)S(1)}, bf16[8,256,256]{2,1,0:T(8,128)(2,1)S(1)}, u32[]{:S(2)}, u32[]{:S(2)}) collective-permute-start(bf16[8,256,256]{2,1,0:T(8,128)(2,1)S(1)} %get-tuple-element.12), channel_id=1, source_target_pairs={{0,1},{1,2},{2,3},{3,4},{4,5},{5,6},{6,7},{7,8},{8,9},{9,10},{10,1... | collective-permute-start | bytes 3145736 | tf_op jit(solution)/shard_map/ppermute | solution.py:387
  44.2 25.5 %collective-permute-start.1 = (bf16[8,256,256]{2,1,0:T(8,128)(2,1)S(1)}, bf16[8,256,256]{2,1,0:T(8,128)(2,1)S(1)}, u32[]{:S(2)}, u32[]{:S(2)}) collective-permute-start(bf16[8,256,256]{2,1,0:T(8,128)(2,1)S(1)} %get-tuple-element.11), channel_id=1, source_target_pairs={{0,15},{1,0},{2,1},{3,2},{4,3},{5,4},{6,5},{7,6},{8,7},{9,8},{10,9... | collective-permute-start | bytes 3145736 | tf_op jit(solution)/shard_map/ppermute | solution.py:387
  67.2 2.5 copy-start
  69.6 1.0 copy-start.1
  82.4 83.8 %all-to-all-start.1 = ((bf16[16,16,4,16,128]{4,3,2,1,0:T(8,128)(2,1)}), bf16[16,16,4,16,128]{4,3,2,1,0:T(8,128)(2,1)}, u32[]{:S(2)}, u32[]{:S(2)}) async-start(bf16[16,16,4,16,128]{4,3,2,1,0:T(8,128)(2,1)} %bitcast.25), calls=%async_computation.1 | async-start | bytes 8388608 | tf_op jit(solution)/shard_map/all_to_all | solution.py:419
  166.2 19.4 %copy-start.2 = (f32[256,256,4]{1,2,0:T(4,128)S(1)}, f32[256,256,4]{1,2,0:T(4,128)}, u32[]{:S(2)}) copy-start(f32[256,256,4]{1,2,0:T(4,128)} %param.14) | copy-start | bytes 3145732
  166.2 97.5 %all-to-all-start = ((bf16[16,16,4,16,128]{4,3,2,1,0:T(8,128)(2,1)}), bf16[16,16,4,16,128]{4,3,2,1,0:T(8,128)(2,1)}, u32[]{:S(2)}, u32[]{:S(2)}) async-start(bf16[16,16,4,16,128]{4,3,2,1,0:T(8,128)(2,1)} %bitcast.24), calls=%async_computation | async-start | bytes 8388608 | tf_op jit(solution)/shard_map/all_to_all | solution.py:419
  277.5 19.4 %copy-start.3 = (f32[8,4,256]{2,1,0:T(4,128)S(1)}, f32[8,4,256]{2,1,0:T(4,128)}, u32[]{:S(2)}) copy-start(f32[8,4,256]{2,1,0:T(4,128)} %get-tuple-element.8) | copy-start | bytes 98308
  277.5 19.4 %copy-start.5 = (f32[4,256]{1,0:T(4,128)S(1)}, f32[4,256]{1,0:T(4,128)}, u32[]{:S(2)}) copy-start(f32[4,256]{1,0:T(4,128)} %get-tuple-element.9) | copy-start | bytes 12292
  277.5 19.4 %copy-start.4 = (f32[8,128]{1,0:T(8,128)S(1)}, f32[8,128]{1,0:T(8,128)}, u32[]{:S(2)}) copy-start(f32[8,128]{1,0:T(8,128)} %get-tuple-element.10) | copy-start | bytes 12292
  277.5 109.3 %all-to-all-start.2 = ((bf16[16,16,4,16,128]{4,3,2,1,0:T(8,128)(2,1)}), bf16[16,16,4,16,128]{4,3,2,1,0:T(8,128)(2,1)}, u32[]{:S(2)}, u32[]{:S(2)}) async-start(bf16[16,16,4,16,128]{4,3,2,1,0:T(8,128)(2,1)} %bitcast.28), calls=%async_computation.2 | async-start | bytes 8388608 | tf_op jit(solution)/shard_map/all_to_all | solution.py:419
  400.0 27.0 %collective-permute-start.2 = (bf16[256,8,128]{2,1,0:T(8,128)(2,1)S(1)}, bf16[256,8,128]{2,1,0:T(8,128)(2,1)S(1)}, u32[]{:S(2)}, u32[]{:S(2)}) collective-permute-start(bf16[256,8,128]{2,1,0:T(8,128)(2,1)S(1)} %get-tuple-element.14), channel_id=1, source_target_pairs={{0,1},{1,2},{2,3},{3,4},{4,5},{5,6},{6,7},{7,8},{8,9},{9,10},{10,1... | collective-permute-start | bytes 1572872 | tf_op jit(solution)/shard_map/ppermute | solution.py:387
  415.2 14.2 %collective-permute-start.3 = (bf16[256,8,128]{2,1,0:T(8,128)(2,1)S(1)}, bf16[256,8,128]{2,1,0:T(8,128)(2,1)S(1)}, u32[]{:S(2)}, u32[]{:S(2)}) collective-permute-start(bf16[256,8,128]{2,1,0:T(8,128)(2,1)S(1)} %get-tuple-element.13), channel_id=1, source_target_pairs={{0,15},{1,0},{2,1},{3,2},{4,3},{5,4},{6,5},{7,6},{8,7},{9,8},{10,9... | collective-permute-start | bytes 1572872 | tf_op jit(solution)/shard_map/ppermute | solution.py:387
  427.0 2.5 copy-start.6
  429.5 0.8 copy-start.7

commit v2 on v1

--- a/solution.py
+++ b/solution.py
@@ -55,16 +55,14 @@
     return jnp.dot(a, b, preferred_element_type=F32)
 
 
-def spread_kernel(group, span, atom_ref, source_ref, weight_ref, out_ref, first, second):
+def spread_kernel(group, span, pitch, atom_ref, source_ref, weight_ref, out_ref, total):
     step = pl.program_id(0)
     atoms = source_ref.shape[0]
     slots = weight_ref.shape[2]
 
     @pl.when(step == 0)
     def _():
-        zero = jnp.zeros((2 * H * span, C), F32)
-        first[0 : 2 * H * span] = zero
-        second[0 : 2 * H * span] = zero
+        total[0 : 2 * H * pitch] = jnp.zeros((2 * H * pitch, C), F32)
 
     lane = lax.broadcasted_iota(jnp.int32, (slots, 128), 1).astype(F32)
     marks = []
@@ -78,43 +76,44 @@
     gathered = dot(jnp.concatenate(marks, axis=0), source_ref[...]).astype(BF)
     for j in range(group):
         ext = dot(weight_ref[j], gathered[j * slots : (j + 1) * slots])
-        base = pl.multiple_of((step * group + j) * (BX * span), 8)
-        for half, total in enumerate((first, second)):
-            part = ext[:, half * C : (half + 1) * C]
-            total[pl.ds(base, 2 * H * span)] += part[: 2 * H * span]
-            total[pl.ds(pl.multiple_of(base + 2 * H * span, 8), BX * span)] = part[2 * H * span :]
+        base = (step * group + j) * (BX * pitch)
+        for x in range(BX + 2 * H):
+            at = pl.ds(pl.multiple_of(base + x * pitch, 8), span)
+            part = ext[x * span : (x + 1) * span]
+            if x < 2 * H:
+                total[at] += part
+            else:
+                total[at] = part
 
     @pl.when(step == pl.num_programs(0) - 1)
     def _():
-        for half, total in enumerate((first, second)):
-            total[NX * span : (NX + H) * span] += total[0 : H * span]
-            total[H * span : 2 * H * span] += total[(NX + H) * span : (NX + 2 * H) * span]
-
-            def move(r, _):
-                out_ref[r, :, half * C : (half + 1) * C] = total[
-                    pl.ds(H * span + r, NX, stride=span), :
-                ].astype(BF)
-                return 0
-
-            lax.fori_loop(0, span, move, 0)
+        total[NX * pitch : (NX + H) * pitch] += total[0 : H * pitch]
+        total[H * pitch : 2 * H * pitch] += total[(NX + H) * pitch : (NX + 2 * H) * pitch]
+
+        def move(r, _):
+            out_ref[r] = total[pl.ds(H * pitch + r, NX, stride=pitch), :].astype(BF)
+            return 0
+
+        lax.fori_loop(0, span, move, 0)
 
 
 def spread(atom_rows, source, weight, span):
     pencils, ext, slots = weight.shape
     group = 4
+    pitch = span + 8
     return pl.pallas_call(
-        functools.partial(spread_kernel, group, span),
+        functools.partial(spread_kernel, group, span, pitch),
         grid=(pencils // group,),
         in_specs=[
             full(atom_rows.shape),
             full(source.shape),
             pl.BlockSpec((group, ext, slots), lambda i: (i, 0, 0)),
         ],
-        out_specs=full((span, NX, 2 * C)),
-        out_shape=jax.ShapeDtypeStruct((span, NX, 2 * C), BF),
-        scratch_shapes=[pltpu.VMEM(((NX + 2 * H) * span, C), F32)] * 2,
+        out_specs=full((span, NX, C)),
+        out_shape=jax.ShapeDtypeStruct((span, NX, C), BF),
+        scratch_shapes=[pltpu.VMEM(((NX + 2 * H) * pitch, C), F32)],
         compiler_params=params(),
-        cost_estimate=pl.CostEstimate(flops=7 * 10**9, bytes_accessed=24 * 10**6, transcendentals=0),
+        cost_estimate=pl.CostEstimate(flops=4 * 10**9, bytes_accessed=14 * 10**6, transcendentals=0),
     )(atom_rows, source, weight)
 
 
@@ -157,14 +156,13 @@
     lax.fori_loop(0, NX // 8, cast, 0)
 
 
-def forward_x(table, ext, below, above, which, y_local):
+def forward_x(table, ext, below, above, y_local):
     span = ext.shape[0]
     inner = y_local * NZ
-    pick = lambda n: pl.BlockSpec((n, NX, C), lambda i: (0, 0, which))
     return pl.pallas_call(
         functools.partial(forward_x_kernel, y_local),
         grid=(1,),
-        in_specs=[full((NX, NX)), pick(span), pick(HR), pick(HR)],
+        in_specs=[full((NX, NX)), full((span, NX, C)), full((HR, NX, C)), full((HR, NX, C))],
         out_specs=full((NX * inner, C)),
         out_shape=jax.ShapeDtypeStruct((NX * inner, C), BF),
         scratch_shapes=[pltpu.VMEM((NX * (inner + 1), C), F32)],
@@ -272,54 +270,58 @@
     )(fwd, inv, flag, gain, filt, last, density, grad)
 
 
-def inverse_x_kernel(y_local, table_ref, in_ref, out_ref, wide, result):
+def inverse_x_kernel(y_local, pitch, starts, count, out_pitch, table_ref, in_ref, *rest):
+    outs, wide, result = rest[:-2], rest[-2], rest[-1]
     inner = y_local * NZ
 
     def widen(i, _):
         for u in range(8):
             k = i * 8 + u
-            wide[pl.ds(k * (inner + 1), inner)] = in_ref[
+            wide[pl.ds(pl.multiple_of(k * pitch, 8), inner)] = in_ref[
                 pl.ds(pl.multiple_of(k * inner, 16), inner)
             ].astype(F32)
         return 0
 
     lax.fori_loop(0, NX // 8, widen, 0)
-
-    def body(i, _):
-        values = []
-        for u in range(2):
-            r = 2 * i + u
-            place = (r % NZ) * y_local + r // NZ
-            values.append(wide[pl.ds(place, NX, stride=inner + 1), :].astype(BF))
-        both = dot(table_ref[...], jnp.concatenate(values, axis=1))
-        result[pl.ds(2 * i, NX, stride=inner + 1), :] = both[:, :C]
-        result[pl.ds(2 * i + 1, NX, stride=inner + 1), :] = both[:, C:]
-        return 0
-
-    lax.fori_loop(0, inner // 2, body, 0)
-
-    def cast(i, _):
-        for u in range(8):
-            x = i * 8 + u
-            out_ref[pl.ds(pl.multiple_of(x * inner, 16), inner)] = result[
-                pl.ds(x * (inner + 1), inner)
-            ].astype(BF)
-        return 0
-
-    lax.fori_loop(0, NX // 8, cast, 0)
-
-
-def inverse_x(table, back, y_local):
-    shape = (NX * y_local * NZ, C)
+    for start, out_ref in zip(starts, outs):
+
+        def body(i, _):
+            values = []
+            for u in range(2):
+                r = start + 2 * i + u
+                place = (r % NZ) * y_local + r // NZ
+                values.append(wide[pl.ds(place, NX, stride=pitch), :].astype(BF))
+            both = dot(table_ref[...], jnp.concatenate(values, axis=1))
+            result[pl.ds(2 * i, NX, stride=out_pitch), :] = both[:, :C]
+            result[pl.ds(2 * i + 1, NX, stride=out_pitch), :] = both[:, C:]
+            return 0
+
+        lax.fori_loop(0, count // 2, body, 0)
+
+        def cast(i, _):
+            for u in range(8):
+                x = i * 8 + u
+                out_ref[x] = result[pl.ds(pl.multiple_of(x * out_pitch, 8), count)].astype(BF)
+            return 0
+
+        lax.fori_loop(0, NX // 8, cast, 0)
+
+
+def inverse_x(table, back, y_local, starts, count):
+    inner = y_local * NZ
+    pitch = inner + 8
+    out_pitch = (count // 8 + 1 - count // 8 % 2) * 8
     return pl.pallas_call(
-        functools.partial(inverse_x_kernel, y_local),
+        functools.partial(inverse_x_kernel, y_local, pitch, starts, count, out_pitch),
         grid=(1,),
-        in_specs=[full((NX, NX)), full(shape)],
-        out_specs=full(shape),
-        out_shape=jax.ShapeDtypeStruct(shape, BF),
-        scratch_shapes=[pltpu.VMEM((NX * (y_local * NZ + 1), C), F32)] * 2,
+        in_specs=[full((NX, NX)), full((NX * inner, C))],
+        out_specs=[full((NX, count, C))] * len(starts),
+        out_shape=[jax.ShapeDtypeStruct((NX, count, C), BF)] * len(starts),
+        scratch_shapes=[pltpu.VMEM((NX * pitch, C), F32), pltpu.VMEM((NX * out_pitch, C), F32)],
         compiler_params=params(),
-        cost_estimate=pl.CostEstimate(flops=10**9, bytes_accessed=8 * 10**6, transcendentals=0),
+        cost_estimate=pl.CostEstimate(
+            flops=10**9 * count * len(starts) // inner, bytes_accessed=8 * 10**6, transcendentals=0
+        ),
     )(table, back)
 
 
@@ -411,9 +413,8 @@
     atom_rows = atom_list.astype(F32)[:, None, :]
     weight = spread_weight.transpose(0, 2, 1)
 
-    ext = spread(atom_rows, jnp.concatenate([charges, cotangent], axis=1), weight, span)
-    below = from_behind(ext[span - HR :], "row", 1)
-    above = from_behind(ext[:HR], "row", -1)
+    def halo(ext):
+        return from_behind(ext[span - HR :], "row", 1), from_behind(ext[:HR], "row", -1)
 
     def exchange(cells):
         return lax.all_to_all(cells, "row", split_axis=0, concat_axis=0, tiled=True)
@@ -425,8 +426,14 @@
             got = got.transpose(1, 2, 3, 0, 4, 5).reshape(1, 2, k_local, NZ, NY, C)
         return got
 
-    density = by_owner(forward_x(fwd_x, ext, below, above, 0, y_local))
-    grad = by_owner(forward_x(fwd_x, ext, below, above, 1, y_local))
+    density_ext = spread(atom_rows, charges, weight, span)
+    density_halo = halo(density_ext)
+    density_ext, later_rows = lax.optimization_barrier((density_ext, atom_rows))
+    grad_ext = spread(later_rows, cotangent, weight, span)
+    grad_halo = halo(grad_ext)
+    density_x = forward_x(fwd_x, density_ext, *density_halo, y_local)
+    density = by_owner(density_x)
+    grad = by_owner(forward_x(fwd_x, grad_ext, *grad_halo, y_local))
 
     own = me * k_local
     filter_modes = filter_modes.transpose(0, 2, 1)
@@ -439,24 +446,28 @@
     back, fgrad, flast, ggrad = modes(
         fwd_y, inv_y, flag, gain[None, :], filt, filter_modes[half], density, grad
     )
-    small = jnp.concatenate([fgrad.reshape(-1, C), flast.reshape(-1, C), ggrad], axis=0)
-    shared = lax.all_gather(small, "row")
+    gains = lax.all_gather(ggrad, "row")
+    half_rows = rows // 2
+    even_first = [(d, d // 2 if d % 2 == 0 else rows - (d + 1) // 2) for d in range(rows)]
+    odd_first = [(d, d // 2 if d % 2 else rows - (d + 2) // 2) for d in range(rows)]
+    single = [(2 * f % rows, rows - f) for f in range(1, half_rows + 1)]
+    near = lax.ppermute(fgrad, "row", even_first)
+    far = lax.ppermute(fgrad, "row", odd_first)
+    edge = lax.ppermute(jnp.where(me == 0, flast, fgrad[0])[None], "row", single)
     if y_local % 16:
         back = back.reshape(2, k_local, NZ, rows, y_local, C).transpose(3, 0, 1, 2, 4, 5)
     back = exchange(back.reshape(rows, 2 * k_local, NZ, y_local, C))
-    rho = inverse_x(inv_x, back.reshape(NX * inner, C), y_local).reshape(NX, inner, C)
-    below = from_behind(rho[:, inner - HR :], "row", 1)
-    above = from_behind(rho[:, :HR], "row", -1)
+    back, gains, near, far, edge = lax.optimization_barrier((back, gains, near, far, edge))
+    gain_grad = jnp.sum(gains[:, 0], axis=0)
+    straight_rows = jnp.concatenate([near, far], axis=0)
+    turned_rows = jnp.concatenate([edge, near[::-1], far[::-1][: k_local - 1]], axis=0)
+    filter_grad = jnp.where(me < half_rows, straight_rows, flip_modes(turned_rows))
+    back = back.reshape(NX * inner, C)
+    head, tail = inverse_x(inv_x, back, y_local, (0, inner - HR), HR)
+    below = from_behind(tail, "row", 1)
+    above = from_behind(head, "row", -1)
+    (rho,) = inverse_x(inv_x, back, y_local, (0,), inner)
     charge_grad = collect(atom_rows, weight, rho, below, above, atoms, span)
-
-    plane = NY * NZ // C
-    body = shared[:, : k_local * plane].reshape(half, NZ, NY)
-    last = shared[0, k_local * plane : (k_local + 1) * plane].reshape(1, NZ, NY)
-    gain_grad = jnp.sum(shared[:, (k_local + 1) * plane], axis=0)
-    known = jnp.concatenate([body, last], axis=0)
-    mine = me * (NX // rows) + jnp.arange(NX // rows)
-    picked = jnp.take(known, jnp.where(mine <= half, mine, NX - mine), axis=0)
-    filter_grad = jnp.where((mine <= half)[:, None, None], picked, flip_modes(picked))
     return (charge_grad, filter_grad.transpose(0, 2, 1), gain_grad)
 
 

time: 448 us -> 431 us (0.962)
  waiting for transfers between devices: 175 us -> 131 us
  starting transfers between devices: 62.4 us -> 90.1 us
  blocking collectives: 88.9 us -> 76.3 us
  Pallas kernels: 100 us -> 111 us
    all_to_all x3, waiting for transfers between devices: 137 us -> 108 us  [exchange(): return lax.all_to_all(cells, 'row', split_axis=0, concat_axis=0, tiled=True)]
    ppermute x4 -> x6, waiting for transfers between devices: 37.8 us -> 22.9 us  [from_behind(): lax.ppermute(value, axis, [(source, (source + steps) % count) for source...]
    all_to_all x3, starting transfers between devices: 44.4 us -> 58.2 us  [exchange(): return lax.all_to_all(cells, 'row', split_axis=0, concat_axis=0, tiled=True)]
    all_gather x1, blocking collectives: 88.9 us -> 76.3 us  [local(): gains = lax.all_gather(ggrad, 'row')]
    pallas_call x2 -> x4, Pallas kernels: 47.5 us -> 57.9 us  [the longest x2 38.3 us: spread(): pl.pallas_call(functools.partial(spread_kernel, group, span, pitch), grid...]
    ppermute x0 -> x3, starting transfers between devices: none -> 8.85 us  [the longest x1 6.12 us: local(): near = lax.ppermute(fgrad, 'row', even_first)]
    ppermute x4 -> x6, starting transfers between devices: 17.9 us -> 23.1 us  [from_behind(): lax.ppermute(value, axis, [(source, (source + steps) % count) for source...]
  transfers between devices with their start and end apart: 7 -> 12, of which waited for: 6 -> 5; matrix products, arithmetic and copies ran while one was open for 2% -> 2% of each run, Pallas kernels for 3% -> 10%
where the time goes in v2:
time: 431 us; the launch traced here: 426 us
  waiting for transfers between devices  131 us (30%)
  Pallas kernels  111 us (26%)
  starting transfers between devices  90.1 us (21%)
  blocking collectives  76.3 us (18%)
  local copies, waits for them, and re-layouts  12.2 us (3%)
  other arithmetic  5 us (1%)
    all_to_all x3, waiting for transfers between devices, exchange(): return lax.all_to_all(cells, 'row', split_axis=0, concat_axis=0, tiled=True)  108 us
    all_gather x1, blocking collectives, local(): gains = lax.all_gather(ggrad, 'row')  76.3 us
    all_to_all x3, starting transfers between devices, exchange(): return lax.all_to_all(cells, 'row', split_axis=0, concat_axis=0, tiled=True)  58.2 us
    pallas_call x2, Pallas kernels, spread(): pl.pallas_call(functools.partial(spread_kernel, group, span, pitch), grid...  38.3 us
    pallas_call x2, Pallas kernels, forward_x(): pl.pallas_call(functools.partial(forward_x_kernel, y_local), grid=(1,), i...  23.5 us
    ppermute x6, starting transfers between devices, from_behind(): lax.ppermute(value, axis, [(source, (source + steps) % count) for source...  23.1 us
    ppermute x6, waiting for transfers between devices, from_behind(): lax.ppermute(value, axis, [(source, (source + steps) % count) for source...  22.9 us
    pallas_call x2, Pallas kernels, inverse_x(): pl.pallas_call(functools.partial(inverse_x_kernel, y_local, pitch, starts...  19.7 us
  transfers between devices with their start and end apart: 12, of which 5 were waited for; matrix products, arithmetic and copies ran while one was open for 2% of the time, Pallas kernels for 10%

profile of v2, /device:TPU:1, one launch (start us, length us, event | category | flops | bytes accessed | tf_op | source)
XLA Modules:
  0.0 426.4 jit_solution(6505139588086933492)
XLA Ops:
  0.6 1.3 convert_element_type.6
  1.9 19.1 %shard_map.121.ext_ref = bf16[80,256,128]{2,1,0:T(8,128)(2,1)} custom-call(f32[32,1,128]{2,1,0:T(1,128)} %bitcast.36, bf16[2048,128]{1,0:T(8,128)(2,1)} %source_ref.2, bf16[32,960,128]{2,1,0:T(8,128)(2,1)} %bitcast.39), custom_call_target="tpu_custom_call" | custom-call | flops 4000000000 | bytes 14000000 | tf_op jit(solution)/shard_map/pallas_call | solution.py:104
  21.1 1.3 fusion.7
  22.5 2.6 collective-permute-start
  25.1 6.8 %collective-permute-done.1.above_ref = bf16[8,256,128]{2,1,0:T(8,128)(2,1)S(1)} collective-permute-done((bf16[8,256,128]{2,1,0:T(8,128)(2,1)S(1)}, bf16[8,256,128]{2,1,0:T(8,128)(2,1)S(1)}, u32[]{:S(2)}, u32[]{:S(2)}) %collective-permute-start.1) | collective-permute-done | bytes 524320 | tf_op jit(solution)/shard_map/ppermute | solution.py:389
  31.9 4.9 %collective-permute-done.below_ref = bf16[8,256,128]{2,1,0:T(8,128)(2,1)S(1)} collective-permute-done((bf16[8,256,128]{2,1,0:T(8,128)(2,1)S(1)}, bf16[8,256,128]{2,1,0:T(8,128)(2,1)S(1)}, u32[]{:S(2)}, u32[]{:S(2)}) %collective-permute-start) | collective-permute-done | bytes 524320 | tf_op jit(solution)/shard_map/ppermute | solution.py:389
  36.9 0.8 copy-done.4
  37.6 11.8 %shard_map.122 = bf16[16384,128]{1,0:T(8,128)(2,1)} custom-call(bf16[256,256]{1,0:T(8,128)(2,1)} %constant.49.clone.table_ref, bf16[80,256,128]{2,1,0:T(8,128)(2,1)} %shard_map.121.ext_ref, bf16[8,256,128]{2,1,0:T(8,128)(2,1)} %copy-done.4, bf16[8,256,128]{2,1,0:T(8,128)(2,1)} %copy-done.2), custom_call_target="tpu_custom_call" | custom-call | flops 1000000000 | bytes 12000000 | tf_op jit(solution)/shard_map/pallas_call | solution.py:162
  49.4 7.2 %all-to-all-start = ((bf16[16,16,4,16,128]{4,3,2,1,0:T(8,128)(2,1)}), bf16[16,16,4,16,128]{4,3,2,1,0:T(8,128)(2,1)}, u32[]{:S(2)}, u32[]{:S(2)}) async-start(bf16[16,16,4,16,128]{4,3,2,1,0:T(8,128)(2,1)} %bitcast.28), calls=%async_computation | async-start | bytes 8388608 | tf_op jit(solution)/shard_map/all_to_all | solution.py:420
  56.7 19.1 %shard_map.123.ext_ref = bf16[80,256,128]{2,1,0:T(8,128)(2,1)} custom-call(f32[32,1,128]{2,1,0:T(1,128)} %bitcast.37, bf16[2048,128]{1,0:T(8,128)(2,1)} %source_ref.3, bf16[32,960,128]{2,1,0:T(8,128)(2,1)} %bitcast.40), custom_call_target="tpu_custom_call" | custom-call | flops 4000000000 | bytes 14000000 | tf_op jit(solution)/shard_map/pallas_call | solution.py:104
  75.8 1.3 fusion.6
  77.3 1.6 collective-permute-start.2
  78.9 11.2 %collective-permute-done.3.above_ref = bf16[8,256,128]{2,1,0:T(8,128)(2,1)S(1)} collective-permute-done((bf16[8,256,128]{2,1,0:T(8,128)(2,1)S(1)}, bf16[8,256,128]{2,1,0:T(8,128)(2,1)S(1)}, u32[]{:S(2)}, u32[]{:S(2)}) %collective-permute-start.3) | collective-permute-done | bytes 524320 | tf_op jit(solution)/shard_map/ppermute | solution.py:389
  90.1 0.8 copy-done.1
  91.7 11.7 %shard_map.124 = bf16[16384,128]{1,0:T(8,128)(2,1)} custom-call(bf16[256,256]{1,0:T(8,128)(2,1)} %constant.49.clone.table_ref, bf16[80,256,128]{2,1,0:T(8,128)(2,1)} %shard_map.123.ext_ref, bf16[8,256,128]{2,1,0:T(8,128)(2,1)} %copy-done.3, bf16[8,256,128]{2,1,0:T(8,128)(2,1)} %copy-done.1), custom_call_target="tpu_custom_call" | custom-call | flops 1000000000 | bytes 12000000 | tf_op jit(solution)/shard_map/pallas_call | solution.py:162
  103.3 37.1 %all-to-all-done = bf16[16,16,4,16,128]{4,3,2,1,0:T(8,128)(2,1)} async-done(((bf16[16,16,4,16,128]{4,3,2,1,0:T(8,128)(2,1)}), bf16[16,16,4,16,128]{4,3,2,1,0:T(8,128)(2,1)}, u32[]{:S(2)}, u32[]{:S(2)}) %all-to-all-start) | async-done | bytes 4194336 | tf_op jit(solution)/shard_map/all_to_all | solution.py:420
  140.4 31.6 %all-to-all-start.1 = ((bf16[16,16,4,16,128]{4,3,2,1,0:T(8,128)(2,1)}), bf16[16,16,4,16,128]{4,3,2,1,0:T(8,128)(2,1)}, u32[]{:S(2)}, u32[]{:S(2)}) async-start(bf16[16,16,4,16,128]{4,3,2,1,0:T(8,128)(2,1)} %bitcast.27), calls=%async_computation.1 | async-start | bytes 8388608 | tf_op jit(solution)/shard_map/all_to_all | solution.py:420
  172.0 0.9 slice.68
  173.5 1.3 reverse.5
  175.5 1.6 pad_maximum_fusion
  179.1 71.0 %all-to-all-done.1 = bf16[16,16,4,16,128]{4,3,2,1,0:T(8,128)(2,1)} async-done(((bf16[16,16,4,16,128]{4,3,2,1,0:T(8,128)(2,1)}), bf16[16,16,4,16,128]{4,3,2,1,0:T(8,128)(2,1)}, u32[]{:S(2)}, u32[]{:S(2)}) %all-to-all-start.1) | async-done | bytes 4194336 | tf_op jit(solution)/shard_map/all_to_all | solution.py:420
  250.6 13.2 %shard_map.125 = (bf16[16,2,8,4,16,128]{5,4,3,2,1,0:T(8,128)(2,1)}, f32[8,4,256]{2,1,0:T(4,128)}, f32[4,256]{1,0:T(4,128)}, f32[8,128]{1,0:T(8,128)}) custom-call(bf16[512,512]{1,0:T(8,128)(2,1)} %constant.51.clone.fwd_ref, bf16[512,512]{1,0:T(8,128)(2,1)} %constant.52.clone.inv_ref, f32[1,128]{1,0:T(1,128)} %broadcast_in_dim.36.flag_ref, ...), custom_call_target="tpu_custom_call" | custom-call | flops 10000000000 | bytes 14000000 | tf_op jit(solution)/shard_map/pallas_call | solution.py:256
  263.9 19.3 %all-to-all-start.2 = ((bf16[16,16,4,16,128]{4,3,2,1,0:T(8,128)(2,1)}), bf16[16,16,4,16,128]{4,3,2,1,0:T(8,128)(2,1)}, u32[]{:S(2)}, u32[]{:S(2)}) async-start(bf16[16,16,4,16,128]{4,3,2,1,0:T(8,128)(2,1)} %bitcast.29), calls=%async_computation.2 | async-start | bytes 8388608 | tf_op jit(solution)/shard_map/all_to_all | solution.py:420
  283.2 2.1 collective-permute-start.5
  285.3 6.1 %collective-permute-start.4 = (f32[8,4,256]{2,1,0:T(4,128)S(1)}, f32[8,4,256]{2,1,0:T(4,128)S(1)}, u32[]{:S(2)}, u32[]{:S(2)}) collective-permute-start(f32[8,4,256]{2,1,0:T(4,128)S(1)} %copy-done.7), channel_id=1, source_target_pairs={{0,0},{1,15},{2,1},{3,14},{4,2},{5,13},{6,3},{7,12},{8,4},{9,11},{... | collective-permute-start | bytes 98312 | tf_op jit(solution)/shard_map/ppermute | solution.py:454
  292.1 76.3 %all-gather = f32[128,128]{1,0:T(8,128)S(1)} all-gather(f32[8,128]{1,0:T(8,128)S(1)} %copy-done.5), channel_id=2, replica_groups=mesh['groups'=2,'row'=16] {'row'}, dimensions={0}, use_global_device_ids=true | all-gather | bytes 69632 | tf_op jit(solution)/shard_map/all_gather | solution.py:449
  368.4 6.4 %shard_map.127 = (bf16[256,8,128]{2,1,0:T(8,128)(2,1)}, bf16[256,8,128]{2,1,0:T(8,128)(2,1)}) custom-call(bf16[256,256]{1,0:T(8,128)(2,1)} %constant.50.clone.table_ref, bf16[16384,128]{1,0:T(8,128)(2,1)} %bitcast.15.in_ref), custom_call_target="tpu_custom_call" | custom-call | flops 250000000 | bytes 8000000 | tf_op jit(solution)/shard_map/pallas_call | solution.py:314
  374.8 18.5 %collective-permute-start.7 = (bf16[256,8,128]{2,1,0:T(8,128)(2,1)}, bf16[256,8,128]{2,1,0:T(8,128)(2,1)S(1)}, u32[]{:S(2)}, u32[]{:S(2)}) collective-permute-start(bf16[256,8,128]{2,1,0:T(8,128)(2,1)} %get-tuple-element.23), channel_id=1, source_target_pairs={{0,1},{1,2},{2,3},{3,4},{4,5},{5,6},{6,7},{7,8},{8,9},{9,10},{10,1... | collective-permute-start | bytes 1572872 | tf_op jit(solution)/shard_map/ppermute | solution.py:389
  393.9 13.3 %shard_map.126.rho_ref = bf16[256,64,128]{2,1,0:T(8,128)(2,1)} custom-call(bf16[256,256]{1,0:T(8,128)(2,1)} %constant.50.clone.table_ref, bf16[16384,128]{1,0:T(8,128)(2,1)} %bitcast.15.in_ref), custom_call_target="tpu_custom_call" | custom-call | flops 1000000000 | bytes 8000000 | tf_op jit(solution)/shard_map/pallas_call | solution.py:314
  408.5 0.8 copy-done.8
  409.3 0.8 copy-done.9
  410.1 16.3 %shard_map.128 = bf16[2048,128]{1,0:T(8,128)(2,1)} custom-call(f32[32,1,128]{2,1,0:T(1,128)} %bitcast.38, bf16[32,960,128]{2,1,0:T(8,128)(2,1)} %bitcast.41, bf16[256,64,128]{2,1,0:T(8,128)(2,1)} %shard_map.126.rho_ref, bf16[256,8,128]{2,1,0:T(8,128)(2,1)} %copy-done.8, bf16[256,8,128]{2,1,0:T(8,128)(2,1)} %copy-done.9), custom_call_target="tpu_custom_call" | custom-call | flops 4000000000 | bytes 14000000 | tf_op jit(solution)/shard_map/pallas_call | solution.py:366
  (47 shorter events, 7.2 us)
Async XLA Ops:
  22.4 9.5 %collective-permute-start.1 = (bf16[8,256,128]{2,1,0:T(8,128)(2,1)S(1)}, bf16[8,256,128]{2,1,0:T(8,128)(2,1)S(1)}, u32[]{:S(2)}, u32[]{:S(2)}) collective-permute-start(bf16[8,256,128]{2,1,0:T(8,128)(2,1)S(1)} %get-tuple-element.31), channel_id=1, source_target_pairs={{0,15},{1,0},{2,1},{3,2},{4,3},{5,4},{6,5},{7,6},{8,7},{9,8},{10,9... | collective-permute-start | bytes 1572872 | tf_op jit(solution)/shard_map/ppermute | solution.py:389
  22.5 14.4 %collective-permute-start = (bf16[8,256,128]{2,1,0:T(8,128)(2,1)S(1)}, bf16[8,256,128]{2,1,0:T(8,128)(2,1)S(1)}, u32[]{:S(2)}, u32[]{:S(2)}) collective-permute-start(bf16[8,256,128]{2,1,0:T(8,128)(2,1)S(1)} %get-tuple-element.32), channel_id=1, source_target_pairs={{0,1},{1,2},{2,3},{3,4},{4,5},{5,6},{6,7},{7,8},{8,9},{9,10},{10,1... | collective-permute-start | bytes 1572872 | tf_op jit(solution)/shard_map/ppermute | solution.py:389
  31.9 4.9 %copy-start.2 = (bf16[8,256,128]{2,1,0:T(8,128)(2,1)}, bf16[8,256,128]{2,1,0:T(8,128)(2,1)S(1)}, u32[]{:S(2)}) copy-start(bf16[8,256,128]{2,1,0:T(8,128)(2,1)S(1)} %collective-permute-done.1.above_ref) | copy-start | bytes 1572868
  36.9 0.8 copy-start.4
  49.4 91.0 %all-to-all-start = ((bf16[16,16,4,16,128]{4,3,2,1,0:T(8,128)(2,1)}), bf16[16,16,4,16,128]{4,3,2,1,0:T(8,128)(2,1)}, u32[]{:S(2)}, u32[]{:S(2)}) async-start(bf16[16,16,4,16,128]{4,3,2,1,0:T(8,128)(2,1)} %bitcast.28), calls=%async_computation | async-start | bytes 8388608 | tf_op jit(solution)/shard_map/all_to_all | solution.py:420
  77.1 13.0 %collective-permute-start.3 = (bf16[8,256,128]{2,1,0:T(8,128)(2,1)S(1)}, bf16[8,256,128]{2,1,0:T(8,128)(2,1)S(1)}, u32[]{:S(2)}, u32[]{:S(2)}) collective-permute-start(bf16[8,256,128]{2,1,0:T(8,128)(2,1)S(1)} %get-tuple-element.29), channel_id=1, source_target_pairs={{0,15},{1,0},{2,1},{3,2},{4,3},{5,4},{6,5},{7,6},{8,7},{9,8},{10,9... | collective-permute-start | bytes 1572872 | tf_op jit(solution)/shard_map/ppermute | solution.py:389
  77.3 12.8 %collective-permute-start.2 = (bf16[8,256,128]{2,1,0:T(8,128)(2,1)S(1)}, bf16[8,256,128]{2,1,0:T(8,128)(2,1)S(1)}, u32[]{:S(2)}, u32[]{:S(2)}) collective-permute-start(bf16[8,256,128]{2,1,0:T(8,128)(2,1)S(1)} %get-tuple-element.30), channel_id=1, source_target_pairs={{0,1},{1,2},{2,3},{3,4},{4,5},{5,6},{6,7},{7,8},{8,9},{9,10},{10,1... | collective-permute-start | bytes 1572872 | tf_op jit(solution)/shard_map/ppermute | solution.py:389
  90.1 0.8 copy-start.1
  90.9 0.8 copy-start.3
  140.4 31.6 %copy-start = (f32[256,256,4]{1,2,0:T(4,128)S(1)}, f32[256,256,4]{1,2,0:T(4,128)}, u32[]{:S(2)}) copy-start(f32[256,256,4]{1,2,0:T(4,128)} %param.14) | copy-start | bytes 3145732
  140.4 109.7 %all-to-all-start.1 = ((bf16[16,16,4,16,128]{4,3,2,1,0:T(8,128)(2,1)}), bf16[16,16,4,16,128]{4,3,2,1,0:T(8,128)(2,1)}, u32[]{:S(2)}, u32[]{:S(2)}) async-start(bf16[16,16,4,16,128]{4,3,2,1,0:T(8,128)(2,1)} %bitcast.27), calls=%async_computation.1 | async-start | bytes 8388608 | tf_op jit(solution)/shard_map/all_to_all | solution.py:420
  263.8 19.3 %copy-start.7 = (f32[8,4,256]{2,1,0:T(4,128)S(1)}, f32[8,4,256]{2,1,0:T(4,128)}, u32[]{:S(2)}) copy-start(f32[8,4,256]{2,1,0:T(4,128)} %get-tuple-element.20) | copy-start | bytes 98308
  263.8 27.5 %copy-start.6 = (f32[4,256]{1,0:T(4,128)S(1)}, f32[4,256]{1,0:T(4,128)}, u32[]{:S(2)}) copy-start(f32[4,256]{1,0:T(4,128)} %get-tuple-element.21) | copy-start | bytes 12292
  263.9 28.2 %copy-start.5 = (f32[8,128]{1,0:T(8,128)S(1)}, f32[8,128]{1,0:T(8,128)}, u32[]{:S(2)}) copy-start(f32[8,128]{1,0:T(8,128)} %get-tuple-element.19) | copy-start | bytes 12292
  263.9 104.6 %all-to-all-start.2 = ((bf16[16,16,4,16,128]{4,3,2,1,0:T(8,128)(2,1)}), bf16[16,16,4,16,128]{4,3,2,1,0:T(8,128)(2,1)}, u32[]{:S(2)}, u32[]{:S(2)}) async-start(bf16[16,16,4,16,128]{4,3,2,1,0:T(8,128)(2,1)} %bitcast.29), calls=%async_computation.2 | async-start | bytes 8388608 | tf_op jit(solution)/shard_map/all_to_all | solution.py:420
  283.2 85.2 %collective-permute-start.5 = (f32[8,4,256]{2,1,0:T(4,128)S(1)}, f32[8,4,256]{2,1,0:T(4,128)S(1)}, u32[]{:S(2)}, u32[]{:S(2)}) collective-permute-start(f32[8,4,256]{2,1,0:T(4,128)S(1)} %copy-done.7), channel_id=1, source_target_pairs={{0,15},{1,0},{2,14},{3,1},{4,13},{5,2},{6,12},{7,3},{8,11},{9,4},{... | collective-permute-start | bytes 98312 | tf_op jit(solution)/shard_map/ppermute | solution.py:455
  285.3 83.2 %collective-permute-start.4 = (f32[8,4,256]{2,1,0:T(4,128)S(1)}, f32[8,4,256]{2,1,0:T(4,128)S(1)}, u32[]{:S(2)}, u32[]{:S(2)}) collective-permute-start(f32[8,4,256]{2,1,0:T(4,128)S(1)} %copy-done.7), channel_id=1, source_target_pairs={{0,0},{1,15},{2,1},{3,14},{4,2},{5,13},{6,3},{7,12},{8,4},{9,11},{... | collective-permute-start | bytes 98312 | tf_op jit(solution)/shard_map/ppermute | solution.py:454
  291.4 77.0 %collective-permute-start.6 = (f32[1,4,256]{2,1,0:T(4,128)S(1)}, f32[1,4,256]{2,1,0:T(4,128)S(1)}, u32[]{:S(2)}, u32[]{:S(2)}) collective-permute-start(f32[1,4,256]{2,1,0:T(4,128)S(1)} %fusion.1), channel_id=1, source_target_pairs={{2,15},{4,14},{6,13},{8,12},{10,11},{12,10},{14,9},{0,8},{18,31},{... | collective-permute-start | bytes 12296 | tf_op jit(solution)/shard_map/ppermute | solution.py:456
  374.8 33.7 %collective-permute-start.7 = (bf16[256,8,128]{2,1,0:T(8,128)(2,1)}, bf16[256,8,128]{2,1,0:T(8,128)(2,1)S(1)}, u32[]{:S(2)}, u32[]{:S(2)}) collective-permute-start(bf16[256,8,128]{2,1,0:T(8,128)(2,1)} %get-tuple-element.23), channel_id=1, source_target_pairs={{0,1},{1,2},{2,3},{3,4},{4,5},{5,6},{6,7},{7,8},{8,9},{9,10},{10,1... | collective-permute-start | bytes 1572872 | tf_op jit(solution)/shard_map/ppermute | solution.py:389
  393.3 15.1 %collective-permute-start.8 = (bf16[256,8,128]{2,1,0:T(8,128)(2,1)}, bf16[256,8,128]{2,1,0:T(8,128)(2,1)S(1)}, u32[]{:S(2)}, u32[]{:S(2)}) collective-permute-start(bf16[256,8,128]{2,1,0:T(8,128)(2,1)} %get-tuple-element.24), channel_id=1, source_target_pairs={{0,15},{1,0},{2,1},{3,2},{4,3},{5,4},{6,5},{7,6},{8,7},{9,8},{10,9... | collective-permute-start | bytes 1572872 | tf_op jit(solution)/shard_map/ppermute | solution.py:389
  408.5 0.8 copy-start.8
  409.3 0.8 copy-start.9
